TPU v7x, 32 devices: a whole 2x2x4 slice. The times are simulated.
32 devices in a mesh: slab: 8 (over z, y), quad: 4 (over x, core).
Axes of the slice: x: 2, y: 2, z: 4, core: 2. Of those that a mesh axis runs over, the one named last changes fastest.
Arguments:
- grain_cell: int32 [4, 262144], P(None, ('slab', 'quad')), may hold values from 0 to 254, as said below
- grain_count: int32 [32], P(('slab', 'quad')), may hold values from 2048 to 8192, as said below
- grain_weight: float32 [262144], P(('slab', 'quad')), may hold values from 0.05 to 0.95
- grain_volume: float32 [262144], P(('slab', 'quad')), may hold values from 0.02 to 0.4
- grain_velocity: float32 [3, 262144], P(None, ('slab', 'quad')), may hold values from -6 to 6
Outputs:
- pressure: float32 [32, 64, 256], P('slab', 'quad')
- drag: float32 [3, 262144], P(None, ('slab', 'quad'))
Inputs may be any that keep to these rules, and one draw needn't show every extreme that they name: grain_cell[0] < 4, grain_cell[1] < 4, grain_cell[2] < 16, grain_cell[3] <= 254; among the slots of one device at most 4096 name the same quarter, and on every device exactly 4096 name one quarter. `grain_count`: some device has all 8192 slots occupied.
All inputs are finite; a program needn't handle non-finite values.
Results may differ from a plain program's by a relative error of at most 0.00002.
Values sent between devices are 32-bit elements; how exact they have to be, the bound alone decides.
No kernel may reach another device: no remote copies, remote signals or barrier semaphores. Data moves between devices by JAX's collectives and lax.ppermute only.
A program may use at most 128 MiB of HBM per device.

v0:
```python
import jax
import jax.numpy as jnp
from jax import lax
from jax.sharding import PartitionSpec as P

CH = 4
CA = 16
CB = 256
ITERS = 12


damping = 0.05
source_gain = 4.0


def extended(block, sides, width):
    for axis, dim in sides:
        count = lax.axis_size(axis)
        forward = [(i, i + 1) for i in range(count - 1)]
        backward = [(target, source) for source, target in forward]
        low = lax.ppermute(
            lax.slice_in_dim(block, block.shape[dim] - width, None, axis=dim), axis, forward
        )
        high = lax.ppermute(lax.slice_in_dim(block, 0, width, axis=dim), axis, backward)
        block = jnp.concatenate([low, block, high], axis=dim)
    return block


def neighbours(padded):
    centre = padded[1:-1, 1:-1]
    along = jnp.pad(centre, ((0, 0), (0, 0), (1, 1)))
    total = padded[2:, 1:-1] + padded[:-2, 1:-1] + padded[1:-1, 2:] + padded[1:-1, :-2]
    return total + along[:, :, 2:] + along[:, :, :-2]


def gradient(wide):
    vel_height = -0.5 * (wide[2:, 1:-1, 1:-1] - wide[:-2, 1:-1, 1:-1])
    vel_across = -0.5 * (wide[1:-1, 2:, 1:-1] - wide[1:-1, :-2, 1:-1])
    vel_along = -0.5 * (wide[1:-1, 1:-1, 2:] - wide[1:-1, 1:-1, :-2])
    return (vel_height, vel_across, vel_along)


def body(grain_cell, grain_count, grain_weight, grain_volume, grain_velocity):
    quarters = lax.axis_size("quad")
    layers, across_cells, along_cells = (CH, CA, CB)
    block = layers * across_cells * along_cells
    slots = jnp.arange(grain_weight.shape[0], dtype=jnp.int32)
    valid = (slots < grain_count[0]).astype(jnp.float32)
    mass = valid * grain_volume
    upper = 1.0 - grain_weight
    target = (
        (grain_cell[0] * layers + grain_cell[1]) * across_cells + grain_cell[2]
    ) * along_cells + grain_cell[3]
    amounts = jnp.stack([mass, mass * grain_velocity[0]])
    partial_value = jnp.zeros((2, quarters * block), jnp.float32)
    partial_value = (
        partial_value.at[:, target]
        .add(amounts * grain_weight)
        .at[:, target + 1]
        .add(amounts * upper)
    )
    partial_value = partial_value.reshape(2, quarters * layers, across_cells, along_cells)
    field = lax.psum_scatter(partial_value, "quad", scatter_dimension=1, tiled=True)
    solid = field[0]
    voidage = 1.0 / (1.0 + solid)
    source = source_gain * field[1]
    start = jnp.zeros((layers, across_cells, along_cells), jnp.float32)
    rimmed = extended(jnp.stack([voidage, source]), (("slab", 1), ("quad", 2)), 1)
    void_wide = rimmed[0]
    source_wide = rimmed[1]

    def relax_twice(repeat, pressure):
        deeper = extended(pressure, (("slab", 0), ("quad", 1)), 2)
        inner = (source_wide + void_wide * neighbours(deeper)) / (6.0 * void_wide + damping)
        return (source + voidage * neighbours(inner)) / (6.0 * voidage + damping)

    pressure = lax.fori_loop(0, ITERS // 2, relax_twice, start)
    rimmed_p = extended(pressure, (("slab", 0), ("quad", 1)), 1)
    vel_height, vel_across, vel_along = gradient(jnp.pad(rimmed_p, ((0, 0), (0, 0), (1, 1))))
    stacked = jnp.stack([vel_height, vel_across, vel_along, solid])
    table = lax.all_gather(stacked, "quad", axis=2, tiled=True)
    across_all = across_cells * quarters
    table = table.reshape(4, layers * across_all * along_cells)
    source_index = (
        grain_cell[1] * across_all + grain_cell[0] * across_cells + grain_cell[2]
    ) * along_cells + grain_cell[3]
    sampled = grain_weight * table[:, source_index] + upper * table[:, source_index + 1]
    factor = mass * (1.0 + sampled[3]) ** 2
    drag = factor * (sampled[:3] - grain_velocity)
    return (pressure, drag)


def solution(mesh):
    placed = (
        P(None, ("slab", "quad")),
        P(("slab", "quad")),
        P(("slab", "quad")),
        P(("slab", "quad")),
        P(None, ("slab", "quad")),
    )
    return jax.shard_map(
        body,
        mesh=mesh,
        in_specs=placed,
        out_specs=(P("slab", "quad", None), P(None, ("slab", "quad"))),
        check_vma=False,
    )
```

profile of v0, /device:TPU:9, one launch (start us, length us, event | category | flops | bytes accessed | tf_op | source)
XLA Modules:
  0.0 469.5 jit_solution(16657282080776549054)
XLA Ops:
  12.5 2.7 copy.19
  15.2 2.7 copy.20
  18.0 57.5 %scatter_custom_fusion = f32[2,65536]{0,1:T(8,128)} fusion(s32[8192]{0:T(1024)S(1)} %bitcast.65, f32[8192,2]{1,0:T(8,128)} %copy.19, f32[]{:T(128)} %constant.46.clone.1), kind=kCustom, calls=%fused_computation.35 | custom fusion | flops 16384 | bytes 524800 | tf_op jit(solution)/shard_map/scatter-add | solution.py:58
  75.5 61.4 %scatter_fusion = f32[2,65536]{0,1:T(8,128)} fusion(f32[2,65536]{0,1:T(8,128)} %scatter_custom_fusion, s32[8192]{0:T(1024)S(1)} %bitcast.62, f32[8192,2]{1,0:T(8,128)} %copy.20), kind=kCustom, calls=%fused_computation.3 | custom fusion | flops 16384 | bytes 229376 | tf_op jit(solution)/shard_map/scatter-add | solution.py:60
  137.0 20.1 %copy.21 = f32[2,16,16,256]{3,2,1,0:T(8,128)} copy(f32[2,16,16,256]{0,3,2,1:T(8,128)} %bitcast.54) | data formatting | bytes 1048576 | tf_op jit(solution)/shard_map/reshape | solution.py:62
  158.4 32.3 %all-reduce.6.cloned.1.call-done = f32[2,16,16,256]{3,2,1,0:T(8,128)} async-done(((f32[2,16,16,256]{3,2,1,0:T(8,128)}), f32[2,16,16,256]{3,2,1,0:T(8,128)}) %all-reduce.6.cloned.1.call-update) | async-done | bytes 524304
  191.6 3.1 collective-permute-start.4
  194.8 3.1 collective-permute-start.5
  199.6 4.8 %collective-permute-start.6 = (f32[2,6,1,256]{3,2,1,0:T(1,128)S(1)}, f32[2,6,1,256]{3,2,1,0:T(1,128)S(1)}, u32[]{:S(2)}, u32[]{:S(2)}) collective-permute-start(f32[2,6,1,256]{3,2,1,0:T(1,128)S(1)} %get-tuple-element.134), channel_id=1, source_target_pairs={{0,1},{1,2},{2,3},{4,5},{5,6},{6,7},{8,9},{9,10},{10,11},{12,13},{... | collective-permute-start | bytes 36872 | tf_op jit(solution)/shard_map/ppermute | solution.py:21
  204.5 1.9 collective-permute-start.7
  206.4 3.1 collective-permute-done.7
  209.6 96.5 %while.13 = (s32[]{:T(128)}, f32[4,16,256]{2,1,0:T(8,128)S(1)}, f32[6,18,256]{2,1,0:T(8,128)S(1)}, f32[6,18,256]{2,1,0:T(8,128)S(1)}, f32[4,16,256]{2,1,0:T(8,12...) while((s32[]{:T(128)}, f32[4,16,256]{2,1,0:T(8,128)S(1)}, ...), condition=%wide.region_4.5_spmd.clone, body=%wide.region_3.4_spmd.clone.sunk | while | flops 802819 | bytes 2851071 | solution.py:77
  209.6 4.0 collective-permute-start
  213.6 1.9 collective-permute-start.1
  215.6 3.6 collective-permute-done.1
  221.1 3.6 collective-permute-start.3
  227.9 3.4 collective-permute-start.1
  231.3 2.2 collective-permute-done.1
  233.5 1.9 collective-permute-start.2
  235.4 5.4 %collective-permute-start.3 = (f32[8,2,256]{2,1,0:T(2,128)S(1)}, f32[8,2,256]{2,1,0:T(2,128)S(1)}, u32[]{:S(2)}, u32[]{:S(2)}) collective-permute-start(f32[8,2,256]{2,1,0:T(2,128)S(1)} %get-tuple-element.194), channel_id=1, source_target_pairs={{0,1},{1,2},{2,3},{4,5},{5,6},{6,7},{8,9},{9,10},{10,11},{12,13},{... | collective-permute-start | bytes 49160 | tf_op jit(solution)/shard_map/while/body/eval_jaxpr/ppermute | solution.py:21
  244.0 3.4 collective-permute-start.1
  247.4 2.2 collective-permute-done.1
  251.5 5.4 %collective-permute-start.3 = (f32[8,2,256]{2,1,0:T(2,128)S(1)}, f32[8,2,256]{2,1,0:T(2,128)S(1)}, u32[]{:S(2)}, u32[]{:S(2)}) collective-permute-start(f32[8,2,256]{2,1,0:T(2,128)S(1)} %get-tuple-element.194), channel_id=1, source_target_pairs={{0,1},{1,2},{2,3},{4,5},{5,6},{6,7},{8,9},{9,10},{10,11},{12,13},{... | collective-permute-start | bytes 49160 | tf_op jit(solution)/shard_map/while/body/eval_jaxpr/ppermute | solution.py:21
  260.0 3.4 collective-permute-start.1
  263.4 2.2 collective-permute-done.1
  267.5 5.4 %collective-permute-start.3 = (f32[8,2,256]{2,1,0:T(2,128)S(1)}, f32[8,2,256]{2,1,0:T(2,128)S(1)}, u32[]{:S(2)}, u32[]{:S(2)}) collective-permute-start(f32[8,2,256]{2,1,0:T(2,128)S(1)} %get-tuple-element.194), channel_id=1, source_target_pairs={{0,1},{1,2},{2,3},{4,5},{5,6},{6,7},{8,9},{9,10},{10,11},{12,13},{... | collective-permute-start | bytes 49160 | tf_op jit(solution)/shard_map/while/body/eval_jaxpr/ppermute | solution.py:21
  274.1 1.9 collective-permute-start
  276.0 3.4 collective-permute-start.1
  279.4 2.2 collective-permute-done.1
  283.5 5.4 %collective-permute-start.3 = (f32[8,2,256]{2,1,0:T(2,128)S(1)}, f32[8,2,256]{2,1,0:T(2,128)S(1)}, u32[]{:S(2)}, u32[]{:S(2)}) collective-permute-start(f32[8,2,256]{2,1,0:T(2,128)S(1)} %get-tuple-element.194), channel_id=1, source_target_pairs={{0,1},{1,2},{2,3},{4,5},{5,6},{6,7},{8,9},{9,10},{10,11},{12,13},{... | collective-permute-start | bytes 49160 | tf_op jit(solution)/shard_map/while/body/eval_jaxpr/ppermute | solution.py:21
  292.1 3.4 collective-permute-start.1
  295.4 2.2 collective-permute-done.1
  299.6 5.4 %collective-permute-start.3 = (f32[8,2,256]{2,1,0:T(2,128)S(1)}, f32[8,2,256]{2,1,0:T(2,128)S(1)}, u32[]{:S(2)}, u32[]{:S(2)}) collective-permute-start(f32[8,2,256]{2,1,0:T(2,128)S(1)} %get-tuple-element.194), channel_id=1, source_target_pairs={{0,1},{1,2},{2,3},{4,5},{5,6},{6,7},{8,9},{9,10},{10,11},{12,13},{... | collective-permute-start | bytes 49160 | tf_op jit(solution)/shard_map/while/body/eval_jaxpr/ppermute | solution.py:21
  306.1 2.7 collective-permute-start.9
  308.9 3.4 collective-permute-start.8
  312.4 2.2 collective-permute-done.8
  316.5 5.5 %collective-permute-start.11 = (f32[6,1,256]{2,1,0:T(1,128)S(1)}, f32[6,1,256]{2,1,0:T(1,128)S(1)}, u32[]{:S(2)}, u32[]{:S(2)}) collective-permute-start(f32[6,1,256]{2,1,0:T(1,128)S(1)} %get-tuple-element.140), channel_id=1, source_target_pairs={{0,1},{1,2},{2,3},{4,5},{5,6},{6,7},{8,9},{9,10},{10,11},{12,13},{... | collective-permute-start | bytes 18440 | tf_op jit(solution)/shard_map/ppermute | solution.py:21
  323.7 20.3 %all-gather.2.cloned.1.call-done = f32[4,4,64,256]{3,2,1,0:T(8,128)} async-done(((f32[4,4,16,256]{3,2,1,0:T(8,128)}), f32[4,4,64,256]{3,2,1,0:T(8,128)}) %all-gather.2.cloned.1.call-update) | async-done | bytes 1048592 | tf_op jit(solution)/shard_map/all_gather | solution.py:81
  344.0 17.7 %copy.22 = f32[4,4,64,256]{0,3,2,1:T(8,128)} copy(f32[4,4,64,256]{3,2,1,0:T(8,128)} %all-gather.2.cloned.1.call-done) | data formatting | bytes 2097152 | tf_op jit(solution)/shard_map/all_gather | solution.py:81
  361.7 38.3 %gather_fusion = f32[8192,4]{1,0:T(8,128)} fusion(f32[4,65536]{0,1:T(8,128)} %bitcast.55, s32[8192]{0:T(1024)S(1)} %broadcast_clamp_fusion.1), kind=kCustom, calls=%fused_computation | custom fusion | bytes 294912 | tf_op jit(solution)/shard_map/gather | solution.py:87
  400.0 38.3 %gather_fusion.1 = f32[8192,4]{1,0:T(8,128)} fusion(f32[4,65536]{0,1:T(8,128)} %bitcast.56, s32[8192]{0:T(1024)S(1)} %broadcast_clamp_fusion), kind=kCustom, calls=%fused_computation.1 | custom fusion | bytes 294912 | tf_op jit(solution)/shard_map/gather | solution.py:87
  438.3 7.0 %add_bitcast_fusion = f32[4,8192]{0,1:T(8,128)S(1)} fusion(f32[8192,4]{1,0:T(8,128)} %gather_fusion.1, f32[8192,4]{1,0:T(8,128)} %gather_fusion, f32[8192]{0:T(1024)S(1)} %broadcast_subtract_fusion, f32[8192]{0:T(1024)S(1)} %copy-done.2), kind=kLoop, calls=%fused_computation.40 | loop fusion | flops 98304 | bytes 458752 | tf_op jit(solution)/shard_map/add | solution.py:87
  445.3 1.9 copy-done
  447.2 2.2 fusion.15
  449.5 2.8 copy.23
  452.4 2.6 copy.24
  455.0 4.1 broadcast_multiply_fusion
  459.2 3.5 copy.25
  (122 shorter events, 36.2 us)
Async XLA Ops:
  7.2 183.5 %all-reduce.6.cloned.1.call-start = ((), (), s32[]{:S(2)}) async-start(), calls=%async_computation.1 | async-start | bytes 1048576
  137.0 20.2 %copy-start.4 = (u32[32]{0:T(128)S(1)}, u32[32]{0:T(128)}, u32[]{:S(2)}) copy-start(u32[32]{0:T(128)} %constant.66) | copy-start | bytes 388
  157.1 186.9 %all-gather.2.cloned.1.call-start = ((), (), s32[]{:S(2)}) async-start(), calls=%async_computation | async-start | bytes 1310720 | tf_op jit(solution)/shard_map/all_gather | solution.py:81
  191.6 6.2 %collective-permute-start.4 = (f32[2,1,16,256]{3,2,1,0:T(8,128)S(1)}, f32[2,1,16,256]{3,2,1,0:T(8,128)S(1)}, u32[]{:S(2)}, u32[]{:S(2)}) collective-permute-start(f32[2,1,16,256]{3,2,1,0:T(8,128)S(1)} %get-tuple-element.138), channel_id=1, source_target_pairs={{0,4},{4,8},{8,12},{12,16},{16,20},{20,24},{24,28},{1,5},{5,9},{9,... | collective-permute-start | bytes 98312 | tf_op jit(solution)/shard_map/ppermute | solution.py:21
  194.8 4.9 %collective-permute-start.5 = (f32[2,1,16,256]{3,2,1,0:T(8,128)S(1)}, f32[2,1,16,256]{3,2,1,0:T(8,128)S(1)}, u32[]{:S(2)}, u32[]{:S(2)}) collective-permute-start(f32[2,1,16,256]{3,2,1,0:T(8,128)S(1)} %get-tuple-element.139), channel_id=1, source_target_pairs={{4,0},{8,4},{12,8},{16,12},{20,16},{24,20},{28,24},{5,1},{9,5},{13... | collective-permute-start | bytes 98312 | tf_op jit(solution)/shard_map/ppermute | solution.py:24
  199.6 6.8 %collective-permute-start.6 = (f32[2,6,1,256]{3,2,1,0:T(1,128)S(1)}, f32[2,6,1,256]{3,2,1,0:T(1,128)S(1)}, u32[]{:S(2)}, u32[]{:S(2)}) collective-permute-start(f32[2,6,1,256]{3,2,1,0:T(1,128)S(1)} %get-tuple-element.134), channel_id=1, source_target_pairs={{0,1},{1,2},{2,3},{4,5},{5,6},{6,7},{8,9},{9,10},{10,11},{12,13},{... | collective-permute-start | bytes 36872 | tf_op jit(solution)/shard_map/ppermute | solution.py:21
  204.5 5.0 %collective-permute-start.7 = (f32[2,6,1,256]{3,2,1,0:T(1,128)S(1)}, f32[2,6,1,256]{3,2,1,0:T(1,128)S(1)}, u32[]{:S(2)}, u32[]{:S(2)}) collective-permute-start(f32[2,6,1,256]{3,2,1,0:T(1,128)S(1)} %get-tuple-element.135), channel_id=1, source_target_pairs={{1,0},{2,1},{3,2},{5,4},{6,5},{7,6},{9,8},{10,9},{11,10},{13,12},{... | collective-permute-start | bytes 36872 | tf_op jit(solution)/shard_map/ppermute | solution.py:24
  209.6 5.9 %collective-permute-start = (f32[2,16,256]{2,1,0:T(8,128)S(1)}, f32[2,16,256]{2,1,0:T(8,128)S(1)}, u32[]{:S(2)}, u32[]{:S(2)}) collective-permute-start(f32[2,16,256]{2,1,0:T(8,128)S(1)} %get-tuple-element.191), channel_id=1, source_target_pairs={{4,0},{8,4},{12,8},{16,12},{20,16},{24,20},{28,24},{5,1},{9,5},{13... | collective-permute-start | bytes 98312 | tf_op jit(solution)/shard_map/while/body/eval_jaxpr/ppermute | solution.py:24
  213.6 5.6 %collective-permute-start.1 = (f32[2,16,256]{2,1,0:T(8,128)S(1)}, f32[2,16,256]{2,1,0:T(8,128)S(1)}, u32[]{:S(2)}, u32[]{:S(2)}) collective-permute-start(f32[2,16,256]{2,1,0:T(8,128)S(1)} %get-tuple-element.192), channel_id=1, source_target_pairs={{0,4},{4,8},{8,12},{12,16},{16,20},{20,24},{24,28},{1,5},{5,9},{9,... | collective-permute-start | bytes 98312 | tf_op jit(solution)/shard_map/while/body/eval_jaxpr/ppermute | solution.py:21
  219.2 5.6 %collective-permute-start.2 = (f32[8,2,256]{2,1,0:T(2,128)S(1)}, f32[8,2,256]{2,1,0:T(2,128)S(1)}, u32[]{:S(2)}, u32[]{:S(2)}) collective-permute-start(f32[8,2,256]{2,1,0:T(2,128)S(1)} %get-tuple-element.193), channel_id=1, source_target_pairs={{1,0},{2,1},{3,2},{5,4},{6,5},{7,6},{9,8},{10,9},{11,10},{13,12},{... | collective-permute-start | bytes 49160 | tf_op jit(solution)/shard_map/while/body/eval_jaxpr/ppermute | solution.py:24
  221.1 4.5 collective-permute-start.3
  226.0 5.3 %collective-permute-start = (f32[2,16,256]{2,1,0:T(8,128)S(1)}, f32[2,16,256]{2,1,0:T(8,128)S(1)}, u32[]{:S(2)}, u32[]{:S(2)}) collective-permute-start(f32[2,16,256]{2,1,0:T(8,128)S(1)} %get-tuple-element.191), channel_id=1, source_target_pairs={{4,0},{8,4},{12,8},{16,12},{20,16},{24,20},{28,24},{5,1},{9,5},{13... | collective-permute-start | bytes 98312 | tf_op jit(solution)/shard_map/while/body/eval_jaxpr/ppermute | solution.py:24
  227.9 5.6 %collective-permute-start.1 = (f32[2,16,256]{2,1,0:T(8,128)S(1)}, f32[2,16,256]{2,1,0:T(8,128)S(1)}, u32[]{:S(2)}, u32[]{:S(2)}) collective-permute-start(f32[2,16,256]{2,1,0:T(8,128)S(1)} %get-tuple-element.192), channel_id=1, source_target_pairs={{0,4},{4,8},{8,12},{12,16},{16,20},{20,24},{24,28},{1,5},{5,9},{9,... | collective-permute-start | bytes 98312 | tf_op jit(solution)/shard_map/while/body/eval_jaxpr/ppermute | solution.py:21
  233.5 7.3 %collective-permute-start.2 = (f32[8,2,256]{2,1,0:T(2,128)S(1)}, f32[8,2,256]{2,1,0:T(2,128)S(1)}, u32[]{:S(2)}, u32[]{:S(2)}) collective-permute-start(f32[8,2,256]{2,1,0:T(2,128)S(1)} %get-tuple-element.193), channel_id=1, source_target_pairs={{1,0},{2,1},{3,2},{5,4},{6,5},{7,6},{9,8},{10,9},{11,10},{13,12},{... | collective-permute-start | bytes 49160 | tf_op jit(solution)/shard_map/while/body/eval_jaxpr/ppermute | solution.py:24
  235.4 6.2 %collective-permute-start.3 = (f32[8,2,256]{2,1,0:T(2,128)S(1)}, f32[8,2,256]{2,1,0:T(2,128)S(1)}, u32[]{:S(2)}, u32[]{:S(2)}) collective-permute-start(f32[8,2,256]{2,1,0:T(2,128)S(1)} %get-tuple-element.194), channel_id=1, source_target_pairs={{0,1},{1,2},{2,3},{4,5},{5,6},{6,7},{8,9},{9,10},{10,11},{12,13},{... | collective-permute-start | bytes 49160 | tf_op jit(solution)/shard_map/while/body/eval_jaxpr/ppermute | solution.py:21
  242.0 5.3 %collective-permute-start = (f32[2,16,256]{2,1,0:T(8,128)S(1)}, f32[2,16,256]{2,1,0:T(8,128)S(1)}, u32[]{:S(2)}, u32[]{:S(2)}) collective-permute-start(f32[2,16,256]{2,1,0:T(8,128)S(1)} %get-tuple-element.191), channel_id=1, source_target_pairs={{4,0},{8,4},{12,8},{16,12},{20,16},{24,20},{28,24},{5,1},{9,5},{13... | collective-permute-start | bytes 98312 | tf_op jit(solution)/shard_map/while/body/eval_jaxpr/ppermute | solution.py:24
  244.0 5.6 %collective-permute-start.1 = (f32[2,16,256]{2,1,0:T(8,128)S(1)}, f32[2,16,256]{2,1,0:T(8,128)S(1)}, u32[]{:S(2)}, u32[]{:S(2)}) collective-permute-start(f32[2,16,256]{2,1,0:T(8,128)S(1)} %get-tuple-element.192), channel_id=1, source_target_pairs={{0,4},{4,8},{8,12},{12,16},{16,20},{20,24},{24,28},{1,5},{5,9},{9,... | collective-permute-start | bytes 98312 | tf_op jit(solution)/shard_map/while/body/eval_jaxpr/ppermute | solution.py:21
  249.5 7.3 %collective-permute-start.2 = (f32[8,2,256]{2,1,0:T(2,128)S(1)}, f32[8,2,256]{2,1,0:T(2,128)S(1)}, u32[]{:S(2)}, u32[]{:S(2)}) collective-permute-start(f32[8,2,256]{2,1,0:T(2,128)S(1)} %get-tuple-element.193), channel_id=1, source_target_pairs={{1,0},{2,1},{3,2},{5,4},{6,5},{7,6},{9,8},{10,9},{11,10},{13,12},{... | collective-permute-start | bytes 49160 | tf_op jit(solution)/shard_map/while/body/eval_jaxpr/ppermute | solution.py:24
  251.5 6.2 %collective-permute-start.3 = (f32[8,2,256]{2,1,0:T(2,128)S(1)}, f32[8,2,256]{2,1,0:T(2,128)S(1)}, u32[]{:S(2)}, u32[]{:S(2)}) collective-permute-start(f32[8,2,256]{2,1,0:T(2,128)S(1)} %get-tuple-element.194), channel_id=1, source_target_pairs={{0,1},{1,2},{2,3},{4,5},{5,6},{6,7},{8,9},{9,10},{10,11},{12,13},{... | collective-permute-start | bytes 49160 | tf_op jit(solution)/shard_map/while/body/eval_jaxpr/ppermute | solution.py:21
  258.1 5.3 %collective-permute-start = (f32[2,16,256]{2,1,0:T(8,128)S(1)}, f32[2,16,256]{2,1,0:T(8,128)S(1)}, u32[]{:S(2)}, u32[]{:S(2)}) collective-permute-start(f32[2,16,256]{2,1,0:T(8,128)S(1)} %get-tuple-element.191), channel_id=1, source_target_pairs={{4,0},{8,4},{12,8},{16,12},{20,16},{24,20},{28,24},{5,1},{9,5},{13... | collective-permute-start | bytes 98312 | tf_op jit(solution)/shard_map/while/body/eval_jaxpr/ppermute | solution.py:24
  260.0 5.6 %collective-permute-start.1 = (f32[2,16,256]{2,1,0:T(8,128)S(1)}, f32[2,16,256]{2,1,0:T(8,128)S(1)}, u32[]{:S(2)}, u32[]{:S(2)}) collective-permute-start(f32[2,16,256]{2,1,0:T(8,128)S(1)} %get-tuple-element.192), channel_id=1, source_target_pairs={{0,4},{4,8},{8,12},{12,16},{16,20},{20,24},{24,28},{1,5},{5,9},{9,... | collective-permute-start | bytes 98312 | tf_op jit(solution)/shard_map/while/body/eval_jaxpr/ppermute | solution.py:21
  265.6 7.3 %collective-permute-start.2 = (f32[8,2,256]{2,1,0:T(2,128)S(1)}, f32[8,2,256]{2,1,0:T(2,128)S(1)}, u32[]{:S(2)}, u32[]{:S(2)}) collective-permute-start(f32[8,2,256]{2,1,0:T(2,128)S(1)} %get-tuple-element.193), channel_id=1, source_target_pairs={{1,0},{2,1},{3,2},{5,4},{6,5},{7,6},{9,8},{10,9},{11,10},{13,12},{... | collective-permute-start | bytes 49160 | tf_op jit(solution)/shard_map/while/body/eval_jaxpr/ppermute | solution.py:24
  267.5 6.2 %collective-permute-start.3 = (f32[8,2,256]{2,1,0:T(2,128)S(1)}, f32[8,2,256]{2,1,0:T(2,128)S(1)}, u32[]{:S(2)}, u32[]{:S(2)}) collective-permute-start(f32[8,2,256]{2,1,0:T(2,128)S(1)} %get-tuple-element.194), channel_id=1, source_target_pairs={{0,1},{1,2},{2,3},{4,5},{5,6},{6,7},{8,9},{9,10},{10,11},{12,13},{... | collective-permute-start | bytes 49160 | tf_op jit(solution)/shard_map/while/body/eval_jaxpr/ppermute | solution.py:21
  274.1 5.3 %collective-permute-start = (f32[2,16,256]{2,1,0:T(8,128)S(1)}, f32[2,16,256]{2,1,0:T(8,128)S(1)}, u32[]{:S(2)}, u32[]{:S(2)}) collective-permute-start(f32[2,16,256]{2,1,0:T(8,128)S(1)} %get-tuple-element.191), channel_id=1, source_target_pairs={{4,0},{8,4},{12,8},{16,12},{20,16},{24,20},{28,24},{5,1},{9,5},{13... | collective-permute-start | bytes 98312 | tf_op jit(solution)/shard_map/while/body/eval_jaxpr/ppermute | solution.py:24
  276.0 5.6 %collective-permute-start.1 = (f32[2,16,256]{2,1,0:T(8,128)S(1)}, f32[2,16,256]{2,1,0:T(8,128)S(1)}, u32[]{:S(2)}, u32[]{:S(2)}) collective-permute-start(f32[2,16,256]{2,1,0:T(8,128)S(1)} %get-tuple-element.192), channel_id=1, source_target_pairs={{0,4},{4,8},{8,12},{12,16},{16,20},{20,24},{24,28},{1,5},{5,9},{9,... | collective-permute-start | bytes 98312 | tf_op jit(solution)/shard_map/while/body/eval_jaxpr/ppermute | solution.py:21
  281.6 7.3 %collective-permute-start.2 = (f32[8,2,256]{2,1,0:T(2,128)S(1)}, f32[8,2,256]{2,1,0:T(2,128)S(1)}, u32[]{:S(2)}, u32[]{:S(2)}) collective-permute-start(f32[8,2,256]{2,1,0:T(2,128)S(1)} %get-tuple-element.193), channel_id=1, source_target_pairs={{1,0},{2,1},{3,2},{5,4},{6,5},{7,6},{9,8},{10,9},{11,10},{13,12},{... | collective-permute-start | bytes 49160 | tf_op jit(solution)/shard_map/while/body/eval_jaxpr/ppermute | solution.py:24
  283.5 6.2 %collective-permute-start.3 = (f32[8,2,256]{2,1,0:T(2,128)S(1)}, f32[8,2,256]{2,1,0:T(2,128)S(1)}, u32[]{:S(2)}, u32[]{:S(2)}) collective-permute-start(f32[8,2,256]{2,1,0:T(2,128)S(1)} %get-tuple-element.194), channel_id=1, source_target_pairs={{0,1},{1,2},{2,3},{4,5},{5,6},{6,7},{8,9},{9,10},{10,11},{12,13},{... | collective-permute-start | bytes 49160 | tf_op jit(solution)/shard_map/while/body/eval_jaxpr/ppermute | solution.py:21
  290.1 5.3 %collective-permute-start = (f32[2,16,256]{2,1,0:T(8,128)S(1)}, f32[2,16,256]{2,1,0:T(8,128)S(1)}, u32[]{:S(2)}, u32[]{:S(2)}) collective-permute-start(f32[2,16,256]{2,1,0:T(8,128)S(1)} %get-tuple-element.191), channel_id=1, source_target_pairs={{4,0},{8,4},{12,8},{16,12},{20,16},{24,20},{28,24},{5,1},{9,5},{13... | collective-permute-start | bytes 98312 | tf_op jit(solution)/shard_map/while/body/eval_jaxpr/ppermute | solution.py:24
  292.1 5.6 %collective-permute-start.1 = (f32[2,16,256]{2,1,0:T(8,128)S(1)}, f32[2,16,256]{2,1,0:T(8,128)S(1)}, u32[]{:S(2)}, u32[]{:S(2)}) collective-permute-start(f32[2,16,256]{2,1,0:T(8,128)S(1)} %get-tuple-element.192), channel_id=1, source_target_pairs={{0,4},{4,8},{8,12},{12,16},{16,20},{20,24},{24,28},{1,5},{5,9},{9,... | collective-permute-start | bytes 98312 | tf_op jit(solution)/shard_map/while/body/eval_jaxpr/ppermute | solution.py:21
  297.6 7.3 %collective-permute-start.2 = (f32[8,2,256]{2,1,0:T(2,128)S(1)}, f32[8,2,256]{2,1,0:T(2,128)S(1)}, u32[]{:S(2)}, u32[]{:S(2)}) collective-permute-start(f32[8,2,256]{2,1,0:T(2,128)S(1)} %get-tuple-element.193), channel_id=1, source_target_pairs={{1,0},{2,1},{3,2},{5,4},{6,5},{7,6},{9,8},{10,9},{11,10},{13,12},{... | collective-permute-start | bytes 49160 | tf_op jit(solution)/shard_map/while/body/eval_jaxpr/ppermute | solution.py:24
  299.6 6.2 %collective-permute-start.3 = (f32[8,2,256]{2,1,0:T(2,128)S(1)}, f32[8,2,256]{2,1,0:T(2,128)S(1)}, u32[]{:S(2)}, u32[]{:S(2)}) collective-permute-start(f32[8,2,256]{2,1,0:T(2,128)S(1)} %get-tuple-element.194), channel_id=1, source_target_pairs={{0,1},{1,2},{2,3},{4,5},{5,6},{6,7},{8,9},{9,10},{10,11},{12,13},{... | collective-permute-start | bytes 49160 | tf_op jit(solution)/shard_map/while/body/eval_jaxpr/ppermute | solution.py:21
  306.1 55.6 %copy-start.1 = (f32[4,16,256]{2,1,0:T(8,128)}, f32[4,16,256]{2,1,0:T(8,128)S(1)}, u32[]{:S(2)}) copy-start(f32[4,16,256]{2,1,0:T(8,128)S(1)} %get-tuple-element.105) | copy-start | bytes 196612
  306.1 6.2 %collective-permute-start.9 = (f32[1,16,256]{2,1,0:T(8,128)S(1)}, f32[1,16,256]{2,1,0:T(8,128)S(1)}, u32[]{:S(2)}, u32[]{:S(2)}) collective-permute-start(f32[1,16,256]{2,1,0:T(8,128)S(1)} %get-tuple-element.145), channel_id=1, source_target_pairs={{0,4},{4,8},{8,12},{12,16},{16,20},{20,24},{24,28},{1,5},{5,9},{9,... | collective-permute-start | bytes 49160 | tf_op jit(solution)/shard_map/ppermute | solution.py:21
  308.9 5.7 %collective-permute-start.8 = (f32[1,16,256]{2,1,0:T(8,128)S(1)}, f32[1,16,256]{2,1,0:T(8,128)S(1)}, u32[]{:S(2)}, u32[]{:S(2)}) collective-permute-start(f32[1,16,256]{2,1,0:T(8,128)S(1)} %get-tuple-element.144), channel_id=1, source_target_pairs={{4,0},{8,4},{12,8},{16,12},{20,16},{24,20},{28,24},{5,1},{9,5},{13... | collective-permute-start | bytes 49160 | tf_op jit(solution)/shard_map/ppermute | solution.py:24
  314.6 7.5 %collective-permute-start.10 = (f32[6,1,256]{2,1,0:T(1,128)S(1)}, f32[6,1,256]{2,1,0:T(1,128)S(1)}, u32[]{:S(2)}, u32[]{:S(2)}) collective-permute-start(f32[6,1,256]{2,1,0:T(1,128)S(1)} %get-tuple-element.141), channel_id=1, source_target_pairs={{1,0},{2,1},{3,2},{5,4},{6,5},{7,6},{9,8},{10,9},{11,10},{13,12},{... | collective-permute-start | bytes 18440 | tf_op jit(solution)/shard_map/ppermute | solution.py:24
  316.5 6.1 %collective-permute-start.11 = (f32[6,1,256]{2,1,0:T(1,128)S(1)}, f32[6,1,256]{2,1,0:T(1,128)S(1)}, u32[]{:S(2)}, u32[]{:S(2)}) collective-permute-start(f32[6,1,256]{2,1,0:T(1,128)S(1)} %get-tuple-element.140), channel_id=1, source_target_pairs={{0,1},{1,2},{2,3},{4,5},{5,6},{6,7},{8,9},{9,10},{10,11},{12,13},{... | collective-permute-start | bytes 18440 | tf_op jit(solution)/shard_map/ppermute | solution.py:21
  323.7 114.6 %copy-start.2 = (f32[8192]{0:T(1024)S(1)}, f32[8192]{0:T(1024)}, u32[]{:S(2)}) copy-start(f32[8192]{0:T(1024)} %param.9) | copy-start | bytes 98308
  445.3 1.9 copy-start
  447.2 5.1 %copy-start.3 = (f32[3,8192]{1,0:T(4,128)S(1)}, f32[3,8192]{1,0:T(4,128)}, u32[]{:S(2)}) copy-start(f32[3,8192]{1,0:T(4,128)} %param.11) | copy-start | bytes 294916
Sparse Core Ops, SparseCore 0:
  157.2 33.4 all-reduce.5
  323.8 20.1 all-gather.1
where the time goes:
time: 473 us; the launch traced here: 469 us
  other arithmetic  140 us (30%)
  local copies, waits for them, and re-layouts  132 us (28%)
  starting transfers between devices  101 us (21%)
  waiting for transfers between devices  79.7 us (17%)
  between operations  15.6 us (3%)
    scatter-add x2, other arithmetic, body(): partial_value = partial_value.at[:, target].add(amounts * grain_weight).a...  119 us
    ppermute x16, starting transfers between devices, extended(): lax.ppermute(lax.slice_in_dim(block, block.shape[dim] - width, None, axis...  65.4 us
    gather x1, local copies, waits for them, and re-layouts, body(): table[:, source_index]  38.3 us
    gather x1, local copies, waits for them, and re-layouts, body(): table[:, source_index + 1]  38.3 us
    ppermute x16, starting transfers between devices, extended(): lax.ppermute(lax.slice_in_dim(block, 0, width, axis=dim), axis, backward)  35.5 us
    unnamed x3, waiting for transfers between devices  32.3 us
    all_gather x1, waiting for transfers between devices, body(): table = lax.all_gather(stacked, 'quad', axis=2, tiled=True)  20.3 us
    reshape x1, local copies, waits for them, and re-layouts, body(): partial_value.reshape(2, quarters * layers, across_cells, along_cells)  20.1 us
  transfers between devices with their start and end apart: 34, of which 18 were waited for; matrix products, arithmetic and copies ran while one was open for 0% of the time, Pallas kernels for 0%

commit v1 on v0

v1 whole, which is shorter than its diff:
```python
import functools

import jax
import jax.numpy as jnp
from jax import lax
from jax.experimental import pallas as pl
from jax.experimental.pallas import tpu as pltpu
from jax.sharding import PartitionSpec as P

CH = 4
CA = 16
CB = 256
ITERS = 12
LANES = 128
DEPTH = -(-ITERS // CH)

damping = 0.05
source_gain = 4.0

VMEM = pl.BlockSpec(memory_space=pltpu.VMEM)
SMEM = pl.BlockSpec(memory_space=pltpu.SMEM)
LIMIT = pltpu.CompilerParams(vmem_limit_bytes=48 * 1024 * 1024)


def halves(value):
    high = value.astype(jnp.bfloat16)
    low = (value - high.astype(jnp.float32)).astype(jnp.bfloat16)
    return high, low


def row_of(cell_ref, span, across):
    return cell_ref[1:2, span] * across + cell_ref[0:1, span] * CA + cell_ref[2:3, span]


def mass_of(count_ref, volume_ref, first, span):
    volume = volume_ref[0:1, span]
    slot = lax.broadcasted_iota(jnp.int32, volume.shape, 1) + first
    return jnp.where(slot < count_ref[0], volume, 0.0)


def deposit_kernel(quads, width, chunk, place_ref, count_ref, cell_ref, weight_ref, volume_ref, velocity_ref, *outs):
    across = quads * CA
    rows = CH * across
    grains = weight_ref.shape[1]
    own = CB // quads
    halo = (width - own) // 2
    row_iota = lax.broadcasted_iota(jnp.int32, (rows, chunk), 0)
    col_iota = lax.broadcasted_iota(jnp.int32, (CB, chunk), 0)
    total = jnp.zeros((4 * CB, rows), jnp.float32)
    for first in range(0, grains, chunk):
        span = pl.ds(first, chunk)
        mass = mass_of(count_ref, volume_ref, first, span)
        moment = mass * velocity_ref[0:1, span]
        lower = weight_ref[0:1, span]
        upper = 1.0 - lower
        row = row_of(cell_ref, span, across)
        hot = jnp.where(row_iota == row, 1.0, 0.0).astype(jnp.bfloat16)
        col = cell_ref[3:4, span]
        at_lower = col_iota == col
        at_upper = col_iota == col + 1
        parts = []
        for amount in (mass, moment):
            low_pieces = halves(amount * lower)
            high_pieces = halves(amount * upper)
            for low, high in zip(low_pieces, high_pieces):
                spread = jnp.where(
                    at_lower,
                    low.astype(jnp.float32),
                    jnp.where(at_upper, high.astype(jnp.float32), 0.0),
                )
                parts.append(spread.astype(jnp.bfloat16))
        spread = jnp.concatenate(parts, axis=0)
        total = total + lax.dot_general(
            spread, hot, (((1,), (1,)), ((), ())), preferred_element_type=jnp.float32
        )
    lane = lax.broadcasted_iota(jnp.int32, (rows, width), 1)
    for field in range(2):
        base = 2 * field * CB
        whole = (total[base : base + CB] + total[base + CB : base + 2 * CB]).T
        for step, out in enumerate(outs):
            target = lax.rem(place_ref[0] + step, quads)
            first = target * own - halo
            moved = pltpu.roll(whole, lax.rem(CB - first, CB), 1)[:, :width]
            column = lane + first
            moved = jnp.where((column >= 0) & (column < CB), moved, 0.0)
            out[field] = moved.reshape(CH, across, width)


def packed(value, own):
    width = value.shape[-1]
    halo = (width - own) // 2
    pieces = width // own
    tall = value.shape[1] // pieces
    lane = lax.broadcasted_iota(jnp.int32, (value.shape[0], tall, width), 2)
    result = None
    for piece in range(pieces):
        part = value[:, piece * tall : (piece + 1) * tall]
        part = pltpu.roll(part, (piece * own - halo) % width, 2)
        result = part if result is None else jnp.where(lane < piece * own, result, part)
    return result


def coefficient_kernel(quads, place_ref, *refs):
    *parts, coef_ref, solid_ref = refs
    own = CB // quads
    width = coef_ref.shape[-1]
    halo = (width - own) // 2
    solid = parts[0][0]
    moment = parts[0][1]
    for part in parts[1:]:
        solid = solid + part[0]
        moment = moment + part[1]
    column = lax.broadcasted_iota(jnp.int32, solid.shape, 2) + (place_ref[0] * own - halo)
    inside = (column >= 0) & (column < CB)
    voidage = 1.0 / (1.0 + solid)
    scale = 1.0 / (6.0 * voidage + damping)
    coef_ref[0] = jnp.where(inside, source_gain * moment * scale, 0.0)
    coef_ref[1] = jnp.where(inside, voidage * scale, 0.0)
    solid_ref[...] = packed(solid, own)


def relax_kernel(quads, solid_ref, *refs):
    *parts, out_ref, offset_ref, gain_ref, even_ref, odd_ref = refs
    own = CB // quads
    layers = CH * len(parts)
    across, width = out_ref.shape[1] * (offset_ref.shape[-1] // own), offset_ref.shape[-1]
    for index, part in enumerate(parts):
        for layer in range(CH):
            offset_ref[index * CH + layer] = part[0, layer]
            gain_ref[index * CH + layer] = part[1, layer]
            even_ref[index * CH + layer] = part[0, layer]
    row = lax.broadcasted_iota(jnp.int32, (across, width), 0)
    old, new = even_ref, odd_ref
    for sweep in range(1, ITERS):

        def one(layer, carry, old=old, new=new):
            centre = old[layer]
            total = old[layer - 1] + old[layer + 1]
            total = total + pltpu.roll(centre, 1, 1) + pltpu.roll(centre, width - 1, 1)
            total = total + jnp.where(row == 0, 0.0, pltpu.roll(centre, 1, 0))
            total = total + jnp.where(row == across - 1, 0.0, pltpu.roll(centre, across - 1, 0))
            new[layer] = offset_ref[layer] + gain_ref[layer] * total
            return carry

        lax.fori_loop(sweep, layers - sweep, one, 0, unroll=2)
        old, new = new, old
    first = DEPTH * CH - 1
    pressure = jnp.stack([old[first + layer] for layer in range(CH + 2)])
    out_ref[: CH + 2] = packed(pressure, own)
    out_ref[CH + 2 :] = solid_ref[...]


def drag_kernel(
    quads, chunk, place_ref, count_ref, cell_ref, weight_ref, volume_ref, velocity_ref, *refs
):
    *parts, pressure_ref, drag_ref, gathered = refs
    across = quads * CA
    rows = CH * across
    own = CB // quads
    grains = weight_ref.shape[1]
    for step, part in enumerate(parts):
        gathered[lax.rem(place_ref[0] + quads - step, quads)] = part[...]
    tall, width = gathered.shape[2:]
    pieces = width // own
    lane = lax.broadcasted_iota(jnp.int32, (2 * CH + 2, tall, width), 2)
    bands = []
    for piece in range(pieces):
        columns = []
        for left in range(0, quads, pieces):
            block = None
            for near in range(pieces):
                part = gathered[left + near]
                if near != piece:
                    part = pltpu.roll(part, ((near - piece) * own) % width, 2)
                block = part if block is None else jnp.where(lane < near * own, block, part)
            columns.append(block)
        bands.append(jnp.concatenate(columns, axis=2))
    table = jnp.concatenate(bands, axis=1)
    pressure = table[: CH + 2]
    solid = table[CH + 2 :]
    centre = pressure[1 : CH + 1]
    gathered_rows = lax.rem(place_ref[0], quads) * CA
    shape = centre.shape
    row = lax.broadcasted_iota(jnp.int32, shape, 1)
    col = lax.broadcasted_iota(jnp.int32, shape, 2)
    after = jnp.where(row == across - 1, 0.0, pltpu.roll(centre, across - 1, 1))
    before = jnp.where(row == 0, 0.0, pltpu.roll(centre, 1, 1))
    right = jnp.where(col == CB - 1, 0.0, pltpu.roll(centre, CB - 1, 2))
    left = jnp.where(col == 0, 0.0, pltpu.roll(centre, 1, 2))
    fields = (
        -0.5 * (pressure[2:] - pressure[:-2]),
        -0.5 * (after - before),
        -0.5 * (right - left),
        solid,
    )
    fields = [field.reshape(rows, CB).T for field in fields]
    high, low = halves(jnp.concatenate(fields, axis=0))
    whole = pltpu.roll(centre, lax.rem(across - gathered_rows, across), 1)
    pressure_ref[...] = whole[:, :CA]

    row_iota = lax.broadcasted_iota(jnp.int32, (rows, chunk), 0)
    col_iota = lax.broadcasted_iota(jnp.int32, (CB, chunk), 0)
    for first in range(0, grains, chunk):
        span = pl.ds(first, chunk)
        mass = mass_of(count_ref, volume_ref, first, span)
        lower = weight_ref[0:1, span]
        upper = 1.0 - lower
        hot = jnp.where(row_iota == row_of(cell_ref, span, across), 1.0, 0.0).astype(jnp.bfloat16)
        at = cell_ref[3:4, span]
        blend = jnp.where(col_iota == at, lower, jnp.where(col_iota == at + 1, upper, 0.0))
        picked = jnp.dot(high, hot, preferred_element_type=jnp.float32) + jnp.dot(
            low, hot, preferred_element_type=jnp.float32
        )
        sampled = [
            jnp.sum(picked[field * CB : (field + 1) * CB] * blend, axis=0, keepdims=True)
            for field in range(4)
        ]
        factor = mass * (1.0 + sampled[3]) ** 2
        for component in range(3):
            drag_ref[component : component + 1, span] = factor * (
                sampled[component] - velocity_ref[component : component + 1, span]
            )


def body(grain_cell, grain_count, grain_weight, grain_volume, grain_velocity):
    quads = lax.axis_size("quad")
    slabs = lax.axis_size("slab")
    grains = grain_weight.shape[0]
    across = quads * CA
    own = CB // quads
    width = -(-(own + 2 * ITERS) // LANES) * LANES
    pieces = width // own
    place = lax.axis_index("quad").astype(jnp.int32).reshape(1)
    weight = grain_weight.reshape(1, grains)
    volume = grain_volume.reshape(1, grains)
    inputs = (place, grain_count, grain_cell, weight, volume, grain_velocity)
    input_specs = [SMEM, SMEM, VMEM, VMEM, VMEM, VMEM]

    windows = pl.pallas_call(
        functools.partial(deposit_kernel, quads, width, min(grains, 1024)),
        out_shape=[jax.ShapeDtypeStruct((2, CH, across, width), jnp.float32)] * quads,
        in_specs=input_specs,
        out_specs=[VMEM] * quads,
        compiler_params=LIMIT,
        name="deposit",
    )(*inputs)

    def turned(step):
        return [(index, (index + step) % quads) for index in range(quads)]

    parts = [windows[0]] + [
        lax.ppermute(windows[step], "quad", turned(step)) for step in range(1, quads)
    ]
    coef, solid = pl.pallas_call(
        functools.partial(coefficient_kernel, quads),
        out_shape=[
            jax.ShapeDtypeStruct((2, CH, across, width), jnp.float32),
            jax.ShapeDtypeStruct((CH, across // pieces, width), jnp.float32),
        ],
        in_specs=[SMEM] + [VMEM] * quads,
        out_specs=[VMEM] * 2,
        compiler_params=LIMIT,
        name="coefficients",
    )(place, *parts)

    def shifted(step):
        return [
            (index, index + step) for index in range(slabs) if 0 <= index + step < slabs
        ]

    stack = [
        coef if step == 0 else lax.ppermute(coef, "slab", shifted(-step))
        for step in range(-DEPTH, DEPTH + 1)
    ]
    layers = CH * len(stack)
    mine = pl.pallas_call(
        functools.partial(relax_kernel, quads),
        out_shape=jax.ShapeDtypeStruct((2 * CH + 2, across // pieces, width), jnp.float32),
        in_specs=[VMEM] * (1 + len(stack)),
        out_specs=VMEM,
        scratch_shapes=[pltpu.VMEM((layers, across, width), jnp.float32)] * 4,
        compiler_params=LIMIT,
        name="relax",
    )(solid, *stack)

    gathered = [mine] + [lax.ppermute(mine, "quad", turned(step)) for step in range(1, quads)]
    pressure, drag = pl.pallas_call(
        functools.partial(drag_kernel, quads, min(grains, 512)),
        out_shape=[
            jax.ShapeDtypeStruct((CH, CA, CB), jnp.float32),
            jax.ShapeDtypeStruct((3, grains), jnp.float32),
        ],
        in_specs=input_specs + [VMEM] * quads,
        out_specs=[VMEM] * 2,
        scratch_shapes=[pltpu.VMEM((quads,) + mine.shape, jnp.float32)],
        compiler_params=LIMIT,
        name="drag",
    )(*inputs, *gathered)
    return pressure, drag


def solution(mesh):
    placed = (
        P(None, ("slab", "quad")),
        P(("slab", "quad")),
        P(("slab", "quad")),
        P(("slab", "quad")),
        P(None, ("slab", "quad")),
    )
    return jax.shard_map(
        body,
        mesh=mesh,
        in_specs=placed,
        out_specs=(P("slab", "quad", None), P(None, ("slab", "quad"))),
        check_vma=False,
    )
```

time: 473 us -> 92.4 us (0.20)
  the two profiles are of different devices: /device:TPU:9 before, /device:TPU:24 now
where the time goes in v1:
time: 92.4 us; the launch traced here: 91.9 us
  waiting for transfers between devices  40.3 us (44%)
  Pallas kernels  28.9 us (31%)
  starting transfers between devices  18 us (19%)
  local copies, waits for them, and re-layouts  3.33 us (4%)
  between operations  1.4 us (2%)
    ppermute x6, waiting for transfers between devices, body(): lax.ppermute(coef, 'slab', shifted(-step))  21.4 us
    ppermute x6, starting transfers between devices, body(): lax.ppermute(coef, 'slab', shifted(-step))  14 us
    pallas_call x1, Pallas kernels, body(): pl.pallas_call(functools.partial(drag_kernel, quads, min(grains, 512)), o...  11.1 us
    ppermute x3, waiting for transfers between devices, body(): lax.ppermute(windows[step], 'quad', turned(step))  10.3 us
    pallas_call x1, Pallas kernels, body(): pl.pallas_call(functools.partial(relax_kernel, quads), out_shape=jax.Shap...  9.56 us
    ppermute x3, waiting for transfers between devices, body(): lax.ppermute(mine, 'quad', turned(step))  8.55 us
    pallas_call x1, Pallas kernels, body(): pl.pallas_call(functools.partial(deposit_kernel, quads, width, min(grains...  8.08 us
    unnamed x16, local copies, waits for them, and re-layouts  3.33 us
  transfers between devices with their start and end apart: 12, of which 9 were waited for; matrix products, arithmetic and copies ran while one was open for 0% of the time, Pallas kernels for 0%

profile of v1, /device:TPU:24, one launch (start us, length us, event | category | flops | bytes accessed | tf_op | source)
XLA Modules:
  0.0 91.9 jit_solution(5325440063380586781)
XLA Ops:
  1.3 0.0 copy-start
  1.3 0.9 copy-done
  2.2 0.0 copy-start.2
  2.2 0.9 copy-done.2
  3.1 0.0 copy-start.4
  3.1 0.8 copy-done.4
  3.8 0.0 copy-start.6
  3.9 0.8 copy-done.6
  4.6 8.1 %deposit.1 = (f32[2,4,64,128]{3,2,1,0:T(8,128)S(1)}, f32[2,4,64,128]{3,2,1,0:T(8,128)S(1)}, f32[2,4,64,128]{3,2,1,0:T(8,128)S(1)}, f32[2,4,64,128]{3,2,1,0:T(8,128)S(1)}) custom-call(s32[1]{0:T(128)} %bitcast.place_ref, s32[1]{0:T(128)S(6)} %copy.7.count_ref, s32[4,8192]{1,0:T(4,128)S(1)} %copy-done, f32[1,8192]{1,0:T(1,128)S(1)} %bitcast.3, ...), custom_call_target="tpu_custom_call" | custom-call | tf_op jit(solution)/shard_map/deposit/pallas_call | solution.py:239
  12.7 0.1 collective-permute-start
  12.8 1.6 %collective-permute-start.1 = (f32[2,4,64,128]{3,2,1,0:T(8,128)S(1)}, f32[2,4,64,128]{3,2,1,0:T(8,128)S(1)}, u32[]{:S(2)}, u32[]{:S(2)}) collective-permute-start(f32[2,4,64,128]{3,2,1,0:T(8,128)S(1)} %get-tuple-element.10), channel_id=1, source_target_pairs={{0,2},{1,3},{2,0},{3,1},{4,6},{5,7},{6,4},{7,5},{8,10},{9,11},{10,... | collective-permute-start | bytes 786440 | tf_op jit(solution)/shard_map/ppermute | solution.py:252
  14.3 1.4 %collective-permute-start.2 = (f32[2,4,64,128]{3,2,1,0:T(8,128)S(1)}, f32[2,4,64,128]{3,2,1,0:T(8,128)S(1)}, u32[]{:S(2)}, u32[]{:S(2)}) collective-permute-start(f32[2,4,64,128]{3,2,1,0:T(8,128)S(1)} %get-tuple-element.11), channel_id=1, source_target_pairs={{0,3},{1,0},{2,1},{3,2},{4,7},{5,4},{6,5},{7,6},{8,11},{9,8},{10,9... | collective-permute-start | bytes 786440 | tf_op jit(solution)/shard_map/ppermute | solution.py:252
  15.7 5.0 %collective-permute-done.refs_1_ = f32[2,4,64,128]{3,2,1,0:T(8,128)S(1)} collective-permute-done((f32[2,4,64,128]{3,2,1,0:T(8,128)S(1)}, f32[2,4,64,128]{3,2,1,0:T(8,128)S(1)}, u32[]{:S(2)}, u32[]{:S(2)}) %collective-permute-start) | collective-permute-done | bytes 262176 | tf_op jit(solution)/shard_map/ppermute | solution.py:252
  20.7 1.2 %collective-permute-done.1.refs_2_ = f32[2,4,64,128]{3,2,1,0:T(8,128)S(1)} collective-permute-done((f32[2,4,64,128]{3,2,1,0:T(8,128)S(1)}, f32[2,4,64,128]{3,2,1,0:T(8,128)S(1)}, u32[]{:S(2)}, u32[]{:S(2)}) %collective-permute-start.1) | collective-permute-done | bytes 262176 | tf_op jit(solution)/shard_map/ppermute | solution.py:252
  22.0 4.0 %collective-permute-done.2.refs_3_ = f32[2,4,64,128]{3,2,1,0:T(8,128)S(1)} collective-permute-done((f32[2,4,64,128]{3,2,1,0:T(8,128)S(1)}, f32[2,4,64,128]{3,2,1,0:T(8,128)S(1)}, u32[]{:S(2)}, u32[]{:S(2)}) %collective-permute-start.2) | collective-permute-done | bytes 262176 | tf_op jit(solution)/shard_map/ppermute | solution.py:252
  26.0 0.1 coefficients.1
  26.1 3.2 %collective-permute-start.8 = (f32[2,4,64,128]{3,2,1,0:T(8,128)S(1)}, f32[2,4,64,128]{3,2,1,0:T(8,128)S(1)}, u32[]{:S(2)}, u32[]{:S(2)}) collective-permute-start(f32[2,4,64,128]{3,2,1,0:T(8,128)S(1)} %get-tuple-element.13.refs_3_), channel_id=1, source_target_pairs={{12,0},{16,4},{20,8},{24,12},{28,16},{13,1},{17,5},{21,9},{25,13},... | collective-permute-start | bytes 786440 | tf_op jit(solution)/shard_map/ppermute | solution.py:272
  29.3 2.4 %collective-permute-start.7 = (f32[2,4,64,128]{3,2,1,0:T(8,128)S(1)}, f32[2,4,64,128]{3,2,1,0:T(8,128)S(1)}, u32[]{:S(2)}, u32[]{:S(2)}) collective-permute-start(f32[2,4,64,128]{3,2,1,0:T(8,128)S(1)} %get-tuple-element.13.refs_3_), channel_id=1, source_target_pairs={{8,0},{12,4},{16,8},{20,12},{24,16},{28,20},{9,1},{13,5},{17,9},{2... | collective-permute-start | bytes 786440 | tf_op jit(solution)/shard_map/ppermute | solution.py:272
  31.7 2.4 %collective-permute-start.6 = (f32[2,4,64,128]{3,2,1,0:T(8,128)S(1)}, f32[2,4,64,128]{3,2,1,0:T(8,128)S(1)}, u32[]{:S(2)}, u32[]{:S(2)}) collective-permute-start(f32[2,4,64,128]{3,2,1,0:T(8,128)S(1)} %get-tuple-element.13.refs_3_), channel_id=1, source_target_pairs={{4,0},{8,4},{12,8},{16,12},{20,16},{24,20},{28,24},{5,1},{9,5},{13... | collective-permute-start | bytes 786440 | tf_op jit(solution)/shard_map/ppermute | solution.py:272
  34.1 3.5 %collective-permute-start.5 = (f32[2,4,64,128]{3,2,1,0:T(8,128)S(1)}, f32[2,4,64,128]{3,2,1,0:T(8,128)S(1)}, u32[]{:S(2)}, u32[]{:S(2)}) collective-permute-start(f32[2,4,64,128]{3,2,1,0:T(8,128)S(1)} %get-tuple-element.13.refs_3_), channel_id=1, source_target_pairs={{0,4},{4,8},{8,12},{12,16},{16,20},{20,24},{24,28},{1,5},{5,9},{9,... | collective-permute-start | bytes 786440 | tf_op jit(solution)/shard_map/ppermute | solution.py:272
  37.6 1.3 %collective-permute-start.4 = (f32[2,4,64,128]{3,2,1,0:T(8,128)S(1)}, f32[2,4,64,128]{3,2,1,0:T(8,128)S(1)}, u32[]{:S(2)}, u32[]{:S(2)}) collective-permute-start(f32[2,4,64,128]{3,2,1,0:T(8,128)S(1)} %get-tuple-element.13.refs_3_), channel_id=1, source_target_pairs={{0,8},{4,12},{8,16},{12,20},{16,24},{20,28},{1,9},{5,13},{9,17},{1... | collective-permute-start | bytes 786440 | tf_op jit(solution)/shard_map/ppermute | solution.py:272
  38.9 0.0 collective-permute-done.8.refs_6_
  38.9 1.3 %collective-permute-start.3 = (f32[2,4,64,128]{3,2,1,0:T(8,128)S(1)}, f32[2,4,64,128]{3,2,1,0:T(8,128)S(1)}, u32[]{:S(2)}, u32[]{:S(2)}) collective-permute-start(f32[2,4,64,128]{3,2,1,0:T(8,128)S(1)} %get-tuple-element.13.refs_3_), channel_id=1, source_target_pairs={{0,12},{4,16},{8,20},{12,24},{16,28},{1,13},{5,17},{9,21},{13,25},... | collective-permute-start | bytes 786440 | tf_op jit(solution)/shard_map/ppermute | solution.py:272
  40.2 1.5 %collective-permute-done.7.refs_5_ = f32[2,4,64,128]{3,2,1,0:T(8,128)S(1)} collective-permute-done((f32[2,4,64,128]{3,2,1,0:T(8,128)S(1)}, f32[2,4,64,128]{3,2,1,0:T(8,128)S(1)}, u32[]{:S(2)}, u32[]{:S(2)}) %collective-permute-start.7) | collective-permute-done | bytes 262176 | tf_op jit(solution)/shard_map/ppermute | solution.py:272
  41.7 7.1 %collective-permute-done.6.refs_4_ = f32[2,4,64,128]{3,2,1,0:T(8,128)S(1)} collective-permute-done((f32[2,4,64,128]{3,2,1,0:T(8,128)S(1)}, f32[2,4,64,128]{3,2,1,0:T(8,128)S(1)}, u32[]{:S(2)}, u32[]{:S(2)}) %collective-permute-start.6) | collective-permute-done | bytes 262176 | tf_op jit(solution)/shard_map/ppermute | solution.py:272
  48.7 0.0 collective-permute-done.5.refs_2_
  48.7 0.0 collective-permute-done.4.refs_1_
  48.7 12.9 %collective-permute-done.3.refs_0_ = f32[2,4,64,128]{3,2,1,0:T(8,128)S(1)} collective-permute-done((f32[2,4,64,128]{3,2,1,0:T(8,128)S(1)}, f32[2,4,64,128]{3,2,1,0:T(8,128)S(1)}, u32[]{:S(2)}, u32[]{:S(2)}) %collective-permute-start.3) | collective-permute-done | bytes 262176 | tf_op jit(solution)/shard_map/ppermute | solution.py:272
  61.6 0.0 copy-start.1
  61.6 0.0 copy-start.3
  61.6 0.0 copy-start.5
  61.6 0.0 copy-start.7
  61.6 9.6 %relax.1.refs_0_ = f32[10,32,128]{2,1,0:T(8,128)S(1)} custom-call(f32[4,32,128]{2,1,0:T(8,128)S(1)} %get-tuple-element.12.solid_ref, f32[2,4,64,128]{3,2,1,0:T(8,128)S(1)} %collective-permute-done.3.refs_0_, f32[2,4,64,128]{3,2,1,0:T(8,128)S(1)} %collective-permute-done.4.refs_1_, f32[2,4,64,128]{3,2,1,0:T(8,128)S(1)} %collective-permute-done.5.refs_2_, ...), custom_call_target="tpu_custom_call" | custom-call | tf_op jit(solution)/shard_map/relax/pallas_call | solution.py:276
  71.2 0.4 collective-permute-start.11
  71.6 0.6 collective-permute-start.10
  72.2 0.0 collective-permute-start.9
  72.2 3.9 %collective-permute-done.11.refs_3_ = f32[10,32,128]{2,1,0:T(8,128)S(1)} collective-permute-done((f32[10,32,128]{2,1,0:T(8,128)S(1)}, f32[10,32,128]{2,1,0:T(8,128)S(1)}, u32[]{:S(2)}, u32[]{:S(2)}) %collective-permute-start.11) | collective-permute-done | bytes 163872 | tf_op jit(solution)/shard_map/ppermute | solution.py:286
  76.2 4.1 %collective-permute-done.10.refs_2_ = f32[10,32,128]{2,1,0:T(8,128)S(1)} collective-permute-done((f32[10,32,128]{2,1,0:T(8,128)S(1)}, f32[10,32,128]{2,1,0:T(8,128)S(1)}, u32[]{:S(2)}, u32[]{:S(2)}) %collective-permute-start.10) | collective-permute-done | bytes 163872 | tf_op jit(solution)/shard_map/ppermute | solution.py:286
  80.2 0.5 collective-permute-done.9.refs_1_
  80.8 0.0 copy-done.1
  80.8 0.0 copy-done.3
  80.8 0.0 copy-done.5
  80.8 0.0 copy-done.7
  80.8 11.1 %drag.1 = (f32[4,16,256]{2,1,0:T(8,128)}, f32[3,8192]{1,0:T(4,128)}) custom-call(s32[1]{0:T(128)} %bitcast.place_ref, s32[1]{0:T(128)S(6)} %copy.7.count_ref, s32[4,8192]{1,0:T(4,128)S(1)} %copy-done.1, f32[1,8192]{1,0:T(1,128)S(1)} %bitcast.4, f32[1,8192]{1,0:T(1,128)S(1)} %bitcast.6, f32[3,8192]{1,0:T(4,128)S(1)} %copy-done.3, ...), custom_call_target="tpu_custom_call" | custom-call | tf_op jit(solution)/shard_map/drag/pallas_call | solution.py:287
Async XLA Ops:
  1.3 0.9 copy-start
  2.2 0.9 copy-start.2
  3.1 0.8 copy-start.4
  3.8 0.8 copy-start.6
  12.7 8.1 %collective-permute-start = (f32[2,4,64,128]{3,2,1,0:T(8,128)S(1)}, f32[2,4,64,128]{3,2,1,0:T(8,128)S(1)}, u32[]{:S(2)}, u32[]{:S(2)}) collective-permute-start(f32[2,4,64,128]{3,2,1,0:T(8,128)S(1)} %get-tuple-element.9), channel_id=1, source_target_pairs={{0,1},{1,2},{2,3},{3,0},{4,5},{5,6},{6,7},{7,4},{8,9},{9,10},{10,1... | collective-permute-start | bytes 786440 | tf_op jit(solution)/shard_map/ppermute | solution.py:252
  12.8 9.2 %collective-permute-start.1 = (f32[2,4,64,128]{3,2,1,0:T(8,128)S(1)}, f32[2,4,64,128]{3,2,1,0:T(8,128)S(1)}, u32[]{:S(2)}, u32[]{:S(2)}) collective-permute-start(f32[2,4,64,128]{3,2,1,0:T(8,128)S(1)} %get-tuple-element.10), channel_id=1, source_target_pairs={{0,2},{1,3},{2,0},{3,1},{4,6},{5,7},{6,4},{7,5},{8,10},{9,11},{10,... | collective-permute-start | bytes 786440 | tf_op jit(solution)/shard_map/ppermute | solution.py:252
  14.3 11.7 %collective-permute-start.2 = (f32[2,4,64,128]{3,2,1,0:T(8,128)S(1)}, f32[2,4,64,128]{3,2,1,0:T(8,128)S(1)}, u32[]{:S(2)}, u32[]{:S(2)}) collective-permute-start(f32[2,4,64,128]{3,2,1,0:T(8,128)S(1)} %get-tuple-element.11), channel_id=1, source_target_pairs={{0,3},{1,0},{2,1},{3,2},{4,7},{5,4},{6,5},{7,6},{8,11},{9,8},{10,9... | collective-permute-start | bytes 786440 | tf_op jit(solution)/shard_map/ppermute | solution.py:252
  26.1 12.8 %collective-permute-start.8 = (f32[2,4,64,128]{3,2,1,0:T(8,128)S(1)}, f32[2,4,64,128]{3,2,1,0:T(8,128)S(1)}, u32[]{:S(2)}, u32[]{:S(2)}) collective-permute-start(f32[2,4,64,128]{3,2,1,0:T(8,128)S(1)} %get-tuple-element.13.refs_3_), channel_id=1, source_target_pairs={{12,0},{16,4},{20,8},{24,12},{28,16},{13,1},{17,5},{21,9},{25,13},... | collective-permute-start | bytes 786440 | tf_op jit(solution)/shard_map/ppermute | solution.py:272
  29.3 12.3 %collective-permute-start.7 = (f32[2,4,64,128]{3,2,1,0:T(8,128)S(1)}, f32[2,4,64,128]{3,2,1,0:T(8,128)S(1)}, u32[]{:S(2)}, u32[]{:S(2)}) collective-permute-start(f32[2,4,64,128]{3,2,1,0:T(8,128)S(1)} %get-tuple-element.13.refs_3_), channel_id=1, source_target_pairs={{8,0},{12,4},{16,8},{20,12},{24,16},{28,20},{9,1},{13,5},{17,9},{2... | collective-permute-start | bytes 786440 | tf_op jit(solution)/shard_map/ppermute | solution.py:272
  31.7 17.0 %collective-permute-start.6 = (f32[2,4,64,128]{3,2,1,0:T(8,128)S(1)}, f32[2,4,64,128]{3,2,1,0:T(8,128)S(1)}, u32[]{:S(2)}, u32[]{:S(2)}) collective-permute-start(f32[2,4,64,128]{3,2,1,0:T(8,128)S(1)} %get-tuple-element.13.refs_3_), channel_id=1, source_target_pairs={{4,0},{8,4},{12,8},{16,12},{20,16},{24,20},{28,24},{5,1},{9,5},{13... | collective-permute-start | bytes 786440 | tf_op jit(solution)/shard_map/ppermute | solution.py:272
  34.1 14.6 %collective-permute-start.5 = (f32[2,4,64,128]{3,2,1,0:T(8,128)S(1)}, f32[2,4,64,128]{3,2,1,0:T(8,128)S(1)}, u32[]{:S(2)}, u32[]{:S(2)}) collective-permute-start(f32[2,4,64,128]{3,2,1,0:T(8,128)S(1)} %get-tuple-element.13.refs_3_), channel_id=1, source_target_pairs={{0,4},{4,8},{8,12},{12,16},{16,20},{20,24},{24,28},{1,5},{5,9},{9,... | collective-permute-start | bytes 786440 | tf_op jit(solution)/shard_map/ppermute | solution.py:272
  37.6 11.1 %collective-permute-start.4 = (f32[2,4,64,128]{3,2,1,0:T(8,128)S(1)}, f32[2,4,64,128]{3,2,1,0:T(8,128)S(1)}, u32[]{:S(2)}, u32[]{:S(2)}) collective-permute-start(f32[2,4,64,128]{3,2,1,0:T(8,128)S(1)} %get-tuple-element.13.refs_3_), channel_id=1, source_target_pairs={{0,8},{4,12},{8,16},{12,20},{16,24},{20,28},{1,9},{5,13},{9,17},{1... | collective-permute-start | bytes 786440 | tf_op jit(solution)/shard_map/ppermute | solution.py:272
  38.9 22.7 %collective-permute-start.3 = (f32[2,4,64,128]{3,2,1,0:T(8,128)S(1)}, f32[2,4,64,128]{3,2,1,0:T(8,128)S(1)}, u32[]{:S(2)}, u32[]{:S(2)}) collective-permute-start(f32[2,4,64,128]{3,2,1,0:T(8,128)S(1)} %get-tuple-element.13.refs_3_), channel_id=1, source_target_pairs={{0,12},{4,16},{8,20},{12,24},{16,28},{1,13},{5,17},{9,21},{13,25},... | collective-permute-start | bytes 786440 | tf_op jit(solution)/shard_map/ppermute | solution.py:272
  61.6 19.2 %copy-start.1 = (s32[4,8192]{1,0:T(4,128)S(1)}, s32[4,8192]{1,0:T(4,128)}, u32[]{:S(2)}) copy-start(s32[4,8192]{1,0:T(4,128)} %cell_ref.3) | copy-start | bytes 393220
  61.6 19.2 %copy-start.3 = (f32[3,8192]{1,0:T(4,128)S(1)}, f32[3,8192]{1,0:T(4,128)}, u32[]{:S(2)}) copy-start(f32[3,8192]{1,0:T(4,128)} %velocity_ref.3) | copy-start | bytes 294916
  61.6 19.2 %copy-start.5 = (f32[8192]{0:T(1024)S(1)}, f32[8192]{0:T(1024)}, u32[]{:S(2)}) copy-start(f32[8192]{0:T(1024)} %param.7) | copy-start | bytes 98308
  61.6 19.2 %copy-start.7 = (f32[8192]{0:T(1024)S(1)}, f32[8192]{0:T(1024)}, u32[]{:S(2)}) copy-start(f32[8192]{0:T(1024)} %param.8) | copy-start | bytes 98308
  71.2 5.0 %collective-permute-start.11 = (f32[10,32,128]{2,1,0:T(8,128)S(1)}, f32[10,32,128]{2,1,0:T(8,128)S(1)}, u32[]{:S(2)}, u32[]{:S(2)}) collective-permute-start(f32[10,32,128]{2,1,0:T(8,128)S(1)} %relax.1.refs_0_), channel_id=1, source_target_pairs={{0,3},{1,0},{2,1},{3,2},{4,7},{5,4},{6,5},{7,6},{8,11},{9,8},{10,9... | collective-permute-start | bytes 491528 | tf_op jit(solution)/shard_map/ppermute | solution.py:286
  71.6 8.6 %collective-permute-start.10 = (f32[10,32,128]{2,1,0:T(8,128)S(1)}, f32[10,32,128]{2,1,0:T(8,128)S(1)}, u32[]{:S(2)}, u32[]{:S(2)}) collective-permute-start(f32[10,32,128]{2,1,0:T(8,128)S(1)} %relax.1.refs_0_), channel_id=1, source_target_pairs={{0,2},{1,3},{2,0},{3,1},{4,6},{5,7},{6,4},{7,5},{8,10},{9,11},{10,... | collective-permute-start | bytes 491528 | tf_op jit(solution)/shard_map/ppermute | solution.py:286
  72.2 8.6 %collective-permute-start.9 = (f32[10,32,128]{2,1,0:T(8,128)S(1)}, f32[10,32,128]{2,1,0:T(8,128)S(1)}, u32[]{:S(2)}, u32[]{:S(2)}) collective-permute-start(f32[10,32,128]{2,1,0:T(8,128)S(1)} %relax.1.refs_0_), channel_id=1, source_target_pairs={{0,1},{1,2},{2,3},{3,0},{4,5},{5,6},{6,7},{7,4},{8,9},{9,10},{10,1... | collective-permute-start | bytes 491528 | tf_op jit(solution)/shard_map/ppermute | solution.py:286

commit v2 on v1

v2 whole, which is shorter than its diff:
```python
import functools

import jax
import jax.numpy as jnp
from jax import lax
from jax.experimental import pallas as pl
from jax.experimental.pallas import tpu as pltpu
from jax.sharding import PartitionSpec as P

CH = 4
CA = 16
CB = 256
ITERS = 12
LANES = 128
SUBLANES = 8
DEPTH = -(-ITERS // CH)

damping = 0.05
source_gain = 4.0

VMEM = pl.BlockSpec(memory_space=pltpu.VMEM)
SMEM = pl.BlockSpec(memory_space=pltpu.SMEM)
HBM = pl.BlockSpec(memory_space=pltpu.HBM)
LIMIT = pltpu.CompilerParams(vmem_limit_bytes=48 * 1024 * 1024)


def reach(distance):
    needed = ITERS - 1 - CH * (max(distance, 1) - 1)
    return 1 << (needed - 1).bit_length()


def lanes_of(shape):
    return lax.broadcasted_iota(jnp.int32, shape, len(shape) - 1)


def turned(value, shift):
    shift %= LANES
    return pltpu.roll(value, shift, value.ndim - 1) if shift else value


def pack_own(window, own):
    pieces = LANES // own
    tall = window.shape[1] // pieces
    lane = lanes_of((window.shape[0], tall, LANES))
    result = window[:, :tall]
    for piece in range(1, pieces):
        part = turned(window[:, piece * tall : (piece + 1) * tall], piece * own)
        result = jnp.where(lane < piece * own, result, part)
    return result


def unpack_own(packed, own):
    pieces = LANES // own
    return jnp.concatenate([turned(packed, -piece * own) for piece in range(pieces)], axis=1)


def strip_plan(across, fields, halo):
    rows = across * 2 * halo // LANES
    return (1, rows) if rows >= SUBLANES else (fields, rows * fields)


def packed_rows(across, fields, halo, own):
    shared, rows = strip_plan(across, fields, halo)
    return fields * CH * across * own // LANES + (fields // shared) * CH * rows


def pack(windows, halo, own):
    across = windows[0].shape[1]
    shared, rows = strip_plan(across, len(windows), halo)
    pieces = [pack_own(window, own) for window in windows]
    lane = lanes_of(windows[0].shape)
    joined = [
        jnp.where(lane >= LANES - halo, window, turned(window, LANES - 2 * halo - own))
        for window in windows
    ]
    lane = lanes_of((CH, rows, LANES))
    for first in range(0, len(windows), shared):
        strip, at = None, 0
        for value in joined[first : first + shared]:
            for row in range(0, across, rows):
                part = turned(value[:, row : row + rows], at + 2 * halo)
                strip = part if strip is None else jnp.where(lane < at, strip, part)
                at += 2 * halo
        pieces.append(strip)
    return jnp.concatenate([piece.reshape(-1, LANES) for piece in pieces], axis=0)


def unpack(value, fields, across, halo, own):
    shared, rows = strip_plan(across, fields, halo)
    tall = across * own // LANES
    count = fields * CH * tall
    owned = value[:count].reshape(fields, CH, tall, LANES)
    strips = value[count:].reshape(fields // shared, CH, rows, LANES)
    lane = lanes_of((CH, rows, LANES))
    windows = []
    for field in range(fields):
        window = unpack_own(owned[field], own)
        strip = strips[field // shared]
        at = (field % shared) * across // rows * 2 * halo
        blocks = []
        for row in range(0, across, rows):
            right = turned(strip, own - at)
            left = turned(strip, -2 * halo - at)
            block = jnp.where(lane < own + halo, right, 0.0)
            block = jnp.where(lane >= LANES - halo, left, block)
            blocks.append(jnp.where(lane < own, window[:, row : row + rows], block))
            at += 2 * halo
        windows.append(jnp.concatenate(blocks, axis=1))
    return windows


def halves(value):
    high = value.astype(jnp.bfloat16)
    low = (value - high.astype(jnp.float32)).astype(jnp.bfloat16)
    return high, low


def short_iota(shape):
    return lax.broadcasted_iota(jnp.int32, shape, 0).astype(jnp.int16)


def row_of(cell_ref, span, across):
    return cell_ref[1:2, span] * across + cell_ref[0:1, span] * CA + cell_ref[2:3, span]


def one_hot(rows, index):
    one, zero = jnp.bfloat16(1), jnp.bfloat16(0)
    return jnp.where(rows == index.astype(jnp.int16), one, zero)


def mass_of(count_ref, volume_ref, first, span):
    volume = volume_ref[0:1, span]
    slot = lax.broadcasted_iota(jnp.int32, volume.shape, 1) + first
    return jnp.where(slot < count_ref[0], volume, 0.0)


def deposit_kernel(quads, chunk, place_ref, count_ref, *refs):
    sources, outs = refs[:4], refs[4 : 4 + quads]
    cell_ref, weight_ref, volume_ref, velocity_ref, sems = refs[4 + quads :]
    copies = [
        pltpu.make_async_copy(source, target, sems.at[index])
        for index, (source, target) in enumerate(
            zip(sources, (cell_ref, weight_ref, volume_ref, velocity_ref))
        )
    ]
    for copy in copies:
        copy.start()
    across = quads * CA
    rows = CH * across
    grains = weight_ref.shape[1]
    own = CB // quads
    row_iota = short_iota((rows, chunk))
    col_iota = short_iota((CB, chunk))
    total = jnp.zeros((4 * CB, rows), jnp.float32)
    for copy in copies:
        copy.wait()
    for first in range(0, grains, chunk):
        span = pl.ds(first, chunk)
        mass = mass_of(count_ref, volume_ref, first, span)
        moment = mass * velocity_ref[0:1, span]
        lower = weight_ref[0:1, span]
        upper = 1.0 - lower
        hot = one_hot(row_iota, row_of(cell_ref, span, across))
        col = cell_ref[3:4, span]
        at_lower = col_iota == col.astype(jnp.int16)
        at_upper = col_iota == (col + 1).astype(jnp.int16)
        parts = []
        for amount in (mass, moment):
            for low, high in zip(halves(amount * lower), halves(amount * upper)):
                parts.append(jnp.where(at_lower, low, jnp.where(at_upper, high, jnp.bfloat16(0))))
        spread = jnp.concatenate(parts, axis=0)
        total = total + lax.dot_general(
            spread, hot, (((1,), (1,)), ((), ())), preferred_element_type=jnp.float32
        )
    lane = lanes_of((CH, across, LANES))
    fields = [
        (total[base : base + CB] + total[base + CB : base + 2 * CB]).T
        for base in range(0, 4 * CB, 2 * CB)
    ]
    for step, out in enumerate(outs):
        target = place_ref[0] ^ step
        windows = []
        for field in fields:
            moved = pltpu.roll(field, lax.rem(CB - target * own, CB), 1)
            moved = moved.reshape(CH, across, CB)
            near, past = moved[:, :, :LANES], moved[:, :, CB - LANES :]
            windows.append(jnp.where(lane < (LANES + own) // 2, near, past))
        out[...] = pack(windows, reach(0), own)


def coefficient_kernel(quads, place_ref, *refs):
    parts, outs, solid_ref = refs[:quads], refs[quads:-1], refs[-1]
    across, own = quads * CA, CB // quads
    total = parts[0][...]
    for part in parts[1:]:
        total = total + part[...]
    solid_ref[...] = total[: solid_ref.shape[0] * solid_ref.shape[1]].reshape(solid_ref.shape)
    solid, moment = unpack(total, 2, across, reach(0), own)
    lane = lanes_of(solid.shape)
    column = jnp.where(lane < (LANES + own) // 2, lane, lane - LANES) + place_ref[0] * own
    inside = (column >= 0) & (column < CB)
    voidage = 1.0 / (1.0 + solid)
    scale = 1.0 / (6.0 * voidage + damping)
    offset = jnp.where(inside, source_gain * moment * scale, 0.0)
    gain = jnp.where(inside, voidage * scale, 0.0)
    for distance, out in enumerate(outs):
        out[...] = pack((offset, gain), reach(distance + 1), own)


def relax_kernel(quads, *refs):
    *parts, out_ref, offset_ref, gain_ref, even_ref, odd_ref = refs
    across, own = quads * CA, CB // quads
    layers = CH * len(parts)
    for index, part in enumerate(parts):
        halo = reach(abs(index - DEPTH))
        span = pl.ds(index * CH, CH)
        offset, gain = unpack(part[...], 2, across, halo, own)
        offset_ref[span] = offset
        even_ref[span] = offset
        gain_ref[span] = gain
    row = lax.broadcasted_iota(jnp.int32, (across, LANES), 0)
    old, new = even_ref, odd_ref
    for sweep in range(1, ITERS):
        for layer in range(sweep, layers - sweep):
            centre = old[layer]
            total = old[layer - 1] + old[layer + 1]
            total = total + turned(centre, 1) + turned(centre, -1)
            total = total + jnp.where(row == 0, 0.0, pltpu.roll(centre, 1, 0))
            total = total + jnp.where(row == across - 1, 0.0, pltpu.roll(centre, across - 1, 0))
            new[layer] = offset_ref[layer] + gain_ref[layer] * total
        old, new = new, old
    first = DEPTH * CH - 1
    out_ref[...] = pack_own(old[first : first + CH + 2], own)


def whole_table(quads, place_ref, parts, gathered):
    own = CB // quads
    pieces = LANES // own
    for step, part in enumerate(parts):
        gathered[place_ref[0] ^ step] = part[...]
    lane = lanes_of(gathered.shape[1:])
    bands = []
    for piece in range(pieces):
        columns = []
        for first in range(0, quads, pieces):
            block = None
            for near in range(pieces):
                part = turned(gathered[first + near], (near - piece) * own)
                block = part if block is None else jnp.where(lane < near * own, block, part)
            columns.append(block)
        bands.append(jnp.concatenate(columns, axis=2))
    return jnp.concatenate(bands, axis=1)


def blend_of(col_iota, cell_ref, weight_ref, span):
    lower = weight_ref[0:1, span]
    at = cell_ref[3:4, span]
    return jnp.where(col_iota == at, lower, jnp.where(col_iota == at + 1, 1.0 - lower, 0.0))


def sample(pieces, hot, blend, fields):
    high, low = pieces
    picked = jnp.dot(high, hot, preferred_element_type=jnp.float32) + jnp.dot(
        low, hot, preferred_element_type=jnp.float32
    )
    return [
        jnp.sum(picked[field * CB : (field + 1) * CB] * blend, axis=0, keepdims=True)
        for field in range(fields)
    ]


def factor_kernel(quads, chunk, place_ref, count_ref, cell_ref, weight_ref, volume_ref, *refs):
    *parts, factor_ref, gathered = refs
    across = quads * CA
    rows = CH * across
    solid = whole_table(quads, place_ref, parts, gathered)
    pieces = halves(solid.reshape(rows, CB).T)
    row_iota = short_iota((rows, chunk))
    col_iota = lax.broadcasted_iota(jnp.int32, (CB, chunk), 0)
    for first in range(0, weight_ref.shape[1], chunk):
        span = pl.ds(first, chunk)
        mass = mass_of(count_ref, volume_ref, first, span)
        hot = one_hot(row_iota, row_of(cell_ref, span, across))
        blend = blend_of(col_iota, cell_ref, weight_ref, span)
        (sampled,) = sample(pieces, hot, blend, 1)
        factor_ref[0:1, span] = mass * (1.0 + sampled) ** 2


def drag_kernel(quads, chunk, place_ref, cell_ref, weight_ref, velocity_ref, factor_ref, *refs):
    *parts, pressure_ref, drag_ref, gathered = refs
    across = quads * CA
    rows = CH * across
    pressure = whole_table(quads, place_ref, parts, gathered)
    centre = pressure[1 : CH + 1]
    shape = centre.shape
    row = lax.broadcasted_iota(jnp.int32, shape, 1)
    col = lax.broadcasted_iota(jnp.int32, shape, 2)
    after = jnp.where(row == across - 1, 0.0, pltpu.roll(centre, across - 1, 1))
    before = jnp.where(row == 0, 0.0, pltpu.roll(centre, 1, 1))
    right = jnp.where(col == CB - 1, 0.0, pltpu.roll(centre, CB - 1, 2))
    left = jnp.where(col == 0, 0.0, pltpu.roll(centre, 1, 2))
    fields = (
        -0.5 * (pressure[2:] - pressure[:-2]),
        -0.5 * (after - before),
        -0.5 * (right - left),
    )
    pieces = halves(jnp.concatenate([field.reshape(rows, CB).T for field in fields], axis=0))
    whole = pltpu.roll(centre, lax.rem(across - place_ref[0] * CA, across), 1)
    pressure_ref[...] = whole[:, :CA]

    row_iota = short_iota((rows, chunk))
    col_iota = lax.broadcasted_iota(jnp.int32, (CB, chunk), 0)
    for first in range(0, weight_ref.shape[1], chunk):
        span = pl.ds(first, chunk)
        hot = one_hot(row_iota, row_of(cell_ref, span, across))
        blend = blend_of(col_iota, cell_ref, weight_ref, span)
        sampled = sample(pieces, hot, blend, 3)
        for component in range(3):
            one = pl.ds(component, 1)
            drag_ref[one, span] = factor_ref[0:1, span] * (
                sampled[component] - velocity_ref[one, span]
            )


def body(grain_cell, grain_count, grain_weight, grain_volume, grain_velocity):
    quads = lax.axis_size("quad")
    slabs = lax.axis_size("slab")
    grains = grain_weight.shape[0]
    across = quads * CA
    own = CB // quads
    tall = across * own // LANES
    place = lax.axis_index("quad").astype(jnp.int32).reshape(1)
    weight = grain_weight.reshape(1, grains)
    volume = grain_volume.reshape(1, grains)

    def cells(*shape):
        return jax.ShapeDtypeStruct(shape, jnp.float32)

    def over_quad(step, value):
        pairs = [(index, index ^ step) for index in range(quads)]
        return lax.ppermute(value, "quad", pairs)

    def over_slab(step, value):
        pairs = [(index, index + step) for index in range(slabs) if 0 <= index + step < slabs]
        return lax.ppermute(value, "slab", pairs)

    windows = pl.pallas_call(
        functools.partial(deposit_kernel, quads, min(grains, 1024)),
        out_shape=[cells(packed_rows(across, 2, reach(0), own), LANES)] * quads,
        in_specs=[SMEM, SMEM] + [HBM] * 4,
        out_specs=[VMEM] * quads,
        scratch_shapes=[
            pltpu.VMEM((4, grains), jnp.int32),
            pltpu.VMEM((1, grains), jnp.float32),
            pltpu.VMEM((1, grains), jnp.float32),
            pltpu.VMEM((3, grains), jnp.float32),
            pltpu.SemaphoreType.DMA((4,)),
        ],
        compiler_params=LIMIT,
        name="deposit",
    )(place, grain_count, grain_cell, weight, volume, grain_velocity)

    parts = [windows[0]] + [over_quad(step, windows[step]) for step in range(1, quads)]
    *coefs, solid = pl.pallas_call(
        functools.partial(coefficient_kernel, quads),
        out_shape=[
            cells(packed_rows(across, 2, reach(distance), own), LANES)
            for distance in range(1, DEPTH + 1)
        ]
        + [cells(CH, tall, LANES)],
        in_specs=[SMEM] + [VMEM] * quads,
        out_specs=[VMEM] * (DEPTH + 1),
        compiler_params=LIMIT,
        name="coefficients",
    )(place, *parts)

    stack = [
        coefs[0] if step == 0 else over_slab(-step, coefs[abs(step) - 1])
        for step in range(-DEPTH, DEPTH + 1)
    ]

    solids = [solid] + [over_quad(step, solid) for step in range(1, quads)]
    factor = pl.pallas_call(
        functools.partial(factor_kernel, quads, min(grains, 1024)),
        out_shape=cells(1, grains),
        in_specs=[SMEM, SMEM] + [VMEM] * (3 + quads),
        out_specs=VMEM,
        scratch_shapes=[pltpu.VMEM((quads,) + solid.shape, jnp.float32)],
        compiler_params=LIMIT,
        cost_estimate=pl.CostEstimate(
            flops=4 * CB * CH * across * grains, bytes_accessed=2**20, transcendentals=0
        ),
        name="factor",
    )(place, grain_count, grain_cell, weight, volume, *solids)

    layers = CH * len(stack)
    mine = pl.pallas_call(
        functools.partial(relax_kernel, quads),
        out_shape=cells(CH + 2, tall, LANES),
        in_specs=[VMEM] * len(stack),
        out_specs=VMEM,
        scratch_shapes=[pltpu.VMEM((layers, across, LANES), jnp.float32)] * 4,
        compiler_params=LIMIT,
        name="relax",
    )(*stack)

    gathered = [mine] + [over_quad(step, mine) for step in range(1, quads)]
    pressure, drag = pl.pallas_call(
        functools.partial(drag_kernel, quads, min(grains, 512)),
        out_shape=[cells(CH, CA, CB), cells(3, grains)],
        in_specs=[SMEM] + [VMEM] * (4 + quads),
        out_specs=[VMEM] * 2,
        scratch_shapes=[pltpu.VMEM((quads,) + mine.shape, jnp.float32)],
        compiler_params=LIMIT,
        name="drag",
    )(place, grain_cell, weight, grain_velocity, factor, *gathered)
    return pressure, drag


def solution(mesh):
    placed = (
        P(None, ("slab", "quad")),
        P(("slab", "quad")),
        P(("slab", "quad")),
        P(("slab", "quad")),
        P(None, ("slab", "quad")),
    )
    return jax.shard_map(
        body,
        mesh=mesh,
        in_specs=placed,
        out_specs=(P("slab", "quad", None), P(None, ("slab", "quad"))),
        check_vma=False,
    )
```

time: 92.4 us -> 69.4 us (0.75)
  the two profiles are of different devices: /device:TPU:24 before, /device:TPU:0 now
where the time goes in v2:
time: 69.4 us; the launch traced here: 69 us
  starting transfers between devices  26.1 us (38%)
  Pallas kernels  22.3 us (32%)
  waiting for transfers between devices  15.8 us (23%)
  local copies, waits for them, and re-layouts  3.34 us (5%)
  between operations  1.46 us (2%)
    ppermute x6, starting transfers between devices, over_slab(): return lax.ppermute(value, 'slab', pairs)  19.1 us
    ppermute x9, waiting for transfers between devices, over_quad(): return lax.ppermute(value, 'quad', pairs)  11.3 us
    pallas_call x1, Pallas kernels, body(): pl.pallas_call(functools.partial(drag_kernel, quads, min(grains, 512)), o...  8.25 us
    ppermute x9, starting transfers between devices, over_quad(): return lax.ppermute(value, 'quad', pairs)  6.99 us
    pallas_call x1, Pallas kernels, body(): pl.pallas_call(functools.partial(deposit_kernel, quads, min(grains, 1024)...  6.19 us
    ppermute x6, waiting for transfers between devices, over_slab(): return lax.ppermute(value, 'slab', pairs)  4.47 us
    pallas_call x1, Pallas kernels, body(): pl.pallas_call(functools.partial(relax_kernel, quads), out_shape=cells(CH...  3.8 us
    pallas_call x1, Pallas kernels, body(): pl.pallas_call(functools.partial(factor_kernel, quads, min(grains, 1024))...  3.36 us
  transfers between devices with their start and end apart: 15, of which 5 were waited for; matrix products, arithmetic and copies ran while one was open for 0% of the time, Pallas kernels for 10%

profile of v2, /device:TPU:0, one launch (start us, length us, event | category | flops | bytes accessed | tf_op | source)
XLA Modules:
  0.0 69.0 jit_solution(88574113180210101)
XLA Ops:
  1.3 0.0 copy-start
  1.3 0.9 %copy-done = s32[4,8192]{1,0:T(4,128)S(1)} copy-done((s32[4,8192]{1,0:T(4,128)S(1)}, s32[4,8192]{1,0:T(4,128)}, u32[]{:S(2)}) %copy-start) | copy-done | bytes 131096
  2.2 0.9 %copy-done.2 = f32[3,8192]{1,0:T(4,128)S(1)} copy-done((f32[3,8192]{1,0:T(4,128)S(1)}, f32[3,8192]{1,0:T(4,128)}, u32[]{:S(2)}) %copy-start.2) | copy-done | bytes 98328
  3.1 0.8 %copy-done.4 = f32[8192]{0:T(1024)S(1)} copy-done((f32[8192]{0:T(1024)S(1)}, f32[8192]{0:T(1024)}, u32[]{:S(2)}) %copy-start.4) | copy-done | bytes 32792
  3.9 0.8 %copy-done.6 = f32[8192]{0:T(1024)S(1)} copy-done((f32[8192]{0:T(1024)S(1)}, f32[8192]{0:T(1024)}, u32[]{:S(2)}) %copy-start.6) | copy-done | bytes 32792
  4.6 6.2 %deposit.1 = (f32[384,128]{1,0:T(8,128)S(1)}, f32[384,128]{1,0:T(8,128)S(1)}, f32[384,128]{1,0:T(8,128)S(1)}, f32[384,128]{1,0:T(8,128)S(1)}) custom-call(s32[1]{0:T(128)} %bitcast.place_ref, s32[1]{0:T(128)S(6)} %copy.7.count_ref, s32[4,8192]{1,0:T(4,128)S(1)} %copy-done, f32[1,8192]{1,0:T(1,128)S(1)} %bitcast.3, f32[1,8192]{1,0:T(1,128)S(1)} %bitcast.6, ...), custom_call_target="tpu_custom_call" | custom-call | tf_op jit(solution)/shard_map/deposit/pallas_call | solution.py:347
  10.8 0.5 collective-permute-start
  11.3 2.6 %collective-permute-start.1 = (f32[384,128]{1,0:T(8,128)S(1)}, f32[384,128]{1,0:T(8,128)S(1)}, u32[]{:S(2)}, u32[]{:S(2)}) collective-permute-start(f32[384,128]{1,0:T(8,128)S(1)} %get-tuple-element.12), channel_id=1, source_target_pairs={{0,2},{1,3},{2,0},{3,1},{4,6},{5,7},{6,4},{7,5},{8,10},{9,11},{10,... | collective-permute-start | bytes 589832 | tf_op jit(solution)/shard_map/ppermute | solution.py:341
  13.9 0.1 collective-permute-start.2
  14.0 0.0 collective-permute-done.refs_1_
  14.0 5.7 %collective-permute-done.1.refs_2_ = f32[384,128]{1,0:T(8,128)S(1)} collective-permute-done((f32[384,128]{1,0:T(8,128)S(1)}, f32[384,128]{1,0:T(8,128)S(1)}, u32[]{:S(2)}, u32[]{:S(2)}) %collective-permute-start.1) | collective-permute-done | bytes 196640 | tf_op jit(solution)/shard_map/ppermute | solution.py:341
  19.6 3.7 %collective-permute-done.2.refs_3_ = f32[384,128]{1,0:T(8,128)S(1)} collective-permute-done((f32[384,128]{1,0:T(8,128)S(1)}, f32[384,128]{1,0:T(8,128)S(1)}, u32[]{:S(2)}, u32[]{:S(2)}) %collective-permute-start.2) | collective-permute-done | bytes 196640 | tf_op jit(solution)/shard_map/ppermute | solution.py:341
  23.3 0.7 %coefficients.1 = (f32[384,128]{1,0:T(8,128)S(1)}, f32[320,128]{1,0:T(8,128)S(1)}, f32[288,128]{1,0:T(8,128)S(1)}, f32[4,32,128]{2,1,0:T(8,128)S(1)}) custom-call(s32[1]{0:T(128)} %bitcast.place_ref, f32[384,128]{1,0:T(8,128)S(1)} %get-tuple-element.10.refs_0_, f32[384,128]{1,0:T(8,128)S(1)} %collective-permute-done.refs_1_, ...), custom_call_target="tpu_custom_call" | custom-call | tf_op jit(solution)/shard_map/coefficients/pallas_call | solution.py:364
  24.0 1.3 %collective-permute-start.11 = (f32[288,128]{1,0:T(8,128)S(1)}, f32[288,128]{1,0:T(8,128)S(1)}, u32[]{:S(2)}, u32[]{:S(2)}) collective-permute-start(f32[288,128]{1,0:T(8,128)S(1)} %get-tuple-element.15), channel_id=1, source_target_pairs={{12,0},{16,4},{20,8},{24,12},{28,16},{13,1},{17,5},{21,9},{25,13},... | collective-permute-start | bytes 442376 | tf_op jit(solution)/shard_map/ppermute | solution.py:345
  25.3 1.3 %collective-permute-start.10 = (f32[320,128]{1,0:T(8,128)S(1)}, f32[320,128]{1,0:T(8,128)S(1)}, u32[]{:S(2)}, u32[]{:S(2)}) collective-permute-start(f32[320,128]{1,0:T(8,128)S(1)} %get-tuple-element.16), channel_id=1, source_target_pairs={{8,0},{12,4},{16,8},{20,12},{24,16},{28,20},{9,1},{13,5},{17,9},{2... | collective-permute-start | bytes 491528 | tf_op jit(solution)/shard_map/ppermute | solution.py:345
  26.6 4.6 %collective-permute-start.7 = (f32[320,128]{1,0:T(8,128)S(1)}, f32[320,128]{1,0:T(8,128)S(1)}, u32[]{:S(2)}, u32[]{:S(2)}) collective-permute-start(f32[320,128]{1,0:T(8,128)S(1)} %get-tuple-element.16), channel_id=1, source_target_pairs={{0,8},{4,12},{8,16},{12,20},{16,24},{20,28},{1,9},{5,13},{9,17},{1... | collective-permute-start | bytes 491528 | tf_op jit(solution)/shard_map/ppermute | solution.py:345
  31.2 5.4 %collective-permute-start.6 = (f32[288,128]{1,0:T(8,128)S(1)}, f32[288,128]{1,0:T(8,128)S(1)}, u32[]{:S(2)}, u32[]{:S(2)}) collective-permute-start(f32[288,128]{1,0:T(8,128)S(1)} %get-tuple-element.15), channel_id=1, source_target_pairs={{0,12},{4,16},{8,20},{12,24},{16,28},{1,13},{5,17},{9,21},{13,25},... | collective-permute-start | bytes 442376 | tf_op jit(solution)/shard_map/ppermute | solution.py:345
  36.7 1.3 %collective-permute-start.9 = (f32[384,128]{1,0:T(8,128)S(1)}, f32[384,128]{1,0:T(8,128)S(1)}, u32[]{:S(2)}, u32[]{:S(2)}) collective-permute-start(f32[384,128]{1,0:T(8,128)S(1)} %get-tuple-element.17.refs_3_), channel_id=1, source_target_pairs={{4,0},{8,4},{12,8},{16,12},{20,16},{24,20},{28,24},{5,1},{9,5},{13... | collective-permute-start | bytes 589832 | tf_op jit(solution)/shard_map/ppermute | solution.py:345
  38.0 0.0 collective-permute-done.11.refs_6_
  38.0 5.2 %collective-permute-start.8 = (f32[384,128]{1,0:T(8,128)S(1)}, f32[384,128]{1,0:T(8,128)S(1)}, u32[]{:S(2)}, u32[]{:S(2)}) collective-permute-start(f32[384,128]{1,0:T(8,128)S(1)} %get-tuple-element.17.refs_3_), channel_id=1, source_target_pairs={{0,4},{4,8},{8,12},{12,16},{16,20},{20,24},{24,28},{1,5},{5,9},{9,... | collective-permute-start | bytes 589832 | tf_op jit(solution)/shard_map/ppermute | solution.py:345
  43.2 0.0 collective-permute-done.6.refs_0_
  43.2 0.0 copy-start.1
  43.2 0.0 copy-start.5
  43.2 0.0 copy-start.7
  43.3 0.1 collective-permute-start.5
  43.3 0.0 collective-permute-done.10.refs_5_
  43.3 1.6 %collective-permute-start.4 = (f32[4,32,128]{2,1,0:T(8,128)S(1)}, f32[4,32,128]{2,1,0:T(8,128)S(1)}, u32[]{:S(2)}, u32[]{:S(2)}) collective-permute-start(f32[4,32,128]{2,1,0:T(8,128)S(1)} %get-tuple-element.14.refs_0_), channel_id=1, source_target_pairs={{0,2},{1,3},{2,0},{3,1},{4,6},{5,7},{6,4},{7,5},{8,10},{9,11},{10,... | collective-permute-start | bytes 196616 | tf_op jit(solution)/shard_map/ppermute | solution.py:341
  44.9 0.0 collective-permute-done.7.refs_1_
  44.9 0.3 collective-permute-start.3
  45.2 0.1 collective-permute-done.9.refs_4_
  45.3 4.4 %collective-permute-done.8.refs_2_ = f32[384,128]{1,0:T(8,128)S(1)} collective-permute-done((f32[384,128]{1,0:T(8,128)S(1)}, f32[384,128]{1,0:T(8,128)S(1)}, u32[]{:S(2)}, u32[]{:S(2)}) %collective-permute-start.8) | collective-permute-done | bytes 196640 | tf_op jit(solution)/shard_map/ppermute | solution.py:345
  49.7 3.8 %relax.1.refs_0_ = f32[6,32,128]{2,1,0:T(8,128)S(1)} custom-call(f32[288,128]{1,0:T(8,128)S(1)} %collective-permute-done.6.refs_0_, f32[320,128]{1,0:T(8,128)S(1)} %collective-permute-done.7.refs_1_, f32[384,128]{1,0:T(8,128)S(1)} %collective-permute-done.8.refs_2_, f32[384,128]{1,0:T(8,128)S(1)} %get-tuple-element.17.refs_3_, ...), custom_call_target="tpu_custom_call" | custom-call | tf_op jit(solution)/shard_map/relax/pallas_call | solution.py:397
  53.5 0.0 copy-start.3
  53.5 1.2 %collective-permute-start.14 = (f32[6,32,128]{2,1,0:T(8,128)S(1)}, f32[6,32,128]{2,1,0:T(8,128)S(1)}, u32[]{:S(2)}, u32[]{:S(2)}) collective-permute-start(f32[6,32,128]{2,1,0:T(8,128)S(1)} %relax.1.refs_0_), channel_id=1, source_target_pairs={{0,3},{1,2},{2,1},{3,0},{4,7},{5,6},{6,5},{7,4},{8,11},{9,10},{10,... | collective-permute-start | bytes 294920 | tf_op jit(solution)/shard_map/ppermute | solution.py:341
  54.6 0.5 collective-permute-start.13
  55.2 0.0 collective-permute-done.5.refs_3_
  55.2 0.2 collective-permute-start.12
  55.4 0.0 collective-permute-done.4.refs_2_
  55.4 0.0 collective-permute-done.3.refs_1_
  55.4 0.0 copy-done.1
  55.4 0.0 copy-done.5
  55.4 0.0 copy-done.7
  55.4 3.4 %factor.1.factor_ref = f32[1,8192]{1,0:T(1,128)S(1)} custom-call(s32[1]{0:T(128)} %bitcast.place_ref, s32[1]{0:T(128)S(6)} %copy.7.count_ref, s32[4,8192]{1,0:T(4,128)S(1)} %copy-done.1, f32[1,8192]{1,0:T(1,128)S(1)} %bitcast.4, f32[1,8192]{1,0:T(1,128)S(1)} %bitcast.7, f32[4,32,128]{2,1,0:T(8,128)S(1)} %get-tuple-element.14.refs_0_, ...), custom_call_target="tpu_custom_call" | custom-call | flops 2147483648 | bytes 1048576 | tf_op jit(solution)/shard_map/factor/pallas_call | solution.py:383
  58.8 0.0 collective-permute-done.14.refs_3_
  58.8 1.9 %collective-permute-done.13.refs_2_ = f32[6,32,128]{2,1,0:T(8,128)S(1)} collective-permute-done((f32[6,32,128]{2,1,0:T(8,128)S(1)}, f32[6,32,128]{2,1,0:T(8,128)S(1)}, u32[]{:S(2)}, u32[]{:S(2)}) %collective-permute-start.13) | collective-permute-done | bytes 98336 | tf_op jit(solution)/shard_map/ppermute | solution.py:341
  60.7 0.0 collective-permute-done.12.refs_1_
  60.7 0.0 copy-done.3
  60.7 8.3 %drag.1 = (f32[4,16,256]{2,1,0:T(8,128)}, f32[3,8192]{1,0:T(4,128)}) custom-call(s32[1]{0:T(128)} %bitcast.place_ref, s32[4,8192]{1,0:T(4,128)S(1)} %copy-done.1, f32[1,8192]{1,0:T(1,128)S(1)} %bitcast.5, f32[3,8192]{1,0:T(4,128)S(1)} %copy-done.3, f32[1,8192]{1,0:T(1,128)S(1)} %factor.1.factor_ref, f32[6,32,128]{2,1,0:T(8,128)S(1)} %relax.1.refs_0_, ...), custom_call_target="tpu_custom_call" | custom-call | tf_op jit(solution)/shard_map/drag/pallas_call | solution.py:408
  (3 shorter events, 0.0 us)
Async XLA Ops:
  1.3 0.9 %copy-start = (s32[4,8192]{1,0:T(4,128)S(1)}, s32[4,8192]{1,0:T(4,128)}, u32[]{:S(2)}) copy-start(s32[4,8192]{1,0:T(4,128)} %cell_ref.3) | copy-start | bytes 393220
  2.2 0.9 %copy-start.2 = (f32[3,8192]{1,0:T(4,128)S(1)}, f32[3,8192]{1,0:T(4,128)}, u32[]{:S(2)}) copy-start(f32[3,8192]{1,0:T(4,128)} %velocity_ref.1) | copy-start | bytes 294916
  3.1 0.8 %copy-start.4 = (f32[8192]{0:T(1024)S(1)}, f32[8192]{0:T(1024)}, u32[]{:S(2)}) copy-start(f32[8192]{0:T(1024)} %param.7) | copy-start | bytes 98308
  3.8 0.8 %copy-start.6 = (f32[8192]{0:T(1024)S(1)}, f32[8192]{0:T(1024)}, u32[]{:S(2)}) copy-start(f32[8192]{0:T(1024)} %param.8) | copy-start | bytes 98308
  10.8 3.2 %collective-permute-start = (f32[384,128]{1,0:T(8,128)S(1)}, f32[384,128]{1,0:T(8,128)S(1)}, u32[]{:S(2)}, u32[]{:S(2)}) collective-permute-start(f32[384,128]{1,0:T(8,128)S(1)} %get-tuple-element.11), channel_id=1, source_target_pairs={{0,1},{1,0},{2,3},{3,2},{4,5},{5,4},{6,7},{7,6},{8,9},{9,8},{10,11... | collective-permute-start | bytes 589832 | tf_op jit(solution)/shard_map/ppermute | solution.py:341
  11.3 8.3 %collective-permute-start.1 = (f32[384,128]{1,0:T(8,128)S(1)}, f32[384,128]{1,0:T(8,128)S(1)}, u32[]{:S(2)}, u32[]{:S(2)}) collective-permute-start(f32[384,128]{1,0:T(8,128)S(1)} %get-tuple-element.12), channel_id=1, source_target_pairs={{0,2},{1,3},{2,0},{3,1},{4,6},{5,7},{6,4},{7,5},{8,10},{9,11},{10,... | collective-permute-start | bytes 589832 | tf_op jit(solution)/shard_map/ppermute | solution.py:341
  13.9 9.4 %collective-permute-start.2 = (f32[384,128]{1,0:T(8,128)S(1)}, f32[384,128]{1,0:T(8,128)S(1)}, u32[]{:S(2)}, u32[]{:S(2)}) collective-permute-start(f32[384,128]{1,0:T(8,128)S(1)} %get-tuple-element.13), channel_id=1, source_target_pairs={{0,3},{1,2},{2,1},{3,0},{4,7},{5,6},{6,5},{7,4},{8,11},{9,10},{10,... | collective-permute-start | bytes 589832 | tf_op jit(solution)/shard_map/ppermute | solution.py:341
  24.0 13.9 %collective-permute-start.11 = (f32[288,128]{1,0:T(8,128)S(1)}, f32[288,128]{1,0:T(8,128)S(1)}, u32[]{:S(2)}, u32[]{:S(2)}) collective-permute-start(f32[288,128]{1,0:T(8,128)S(1)} %get-tuple-element.15), channel_id=1, source_target_pairs={{12,0},{16,4},{20,8},{24,12},{28,16},{13,1},{17,5},{21,9},{25,13},... | collective-permute-start | bytes 442376 | tf_op jit(solution)/shard_map/ppermute | solution.py:345
  25.3 18.0 %collective-permute-start.10 = (f32[320,128]{1,0:T(8,128)S(1)}, f32[320,128]{1,0:T(8,128)S(1)}, u32[]{:S(2)}, u32[]{:S(2)}) collective-permute-start(f32[320,128]{1,0:T(8,128)S(1)} %get-tuple-element.16), channel_id=1, source_target_pairs={{8,0},{12,4},{16,8},{20,12},{24,16},{28,20},{9,1},{13,5},{17,9},{2... | collective-permute-start | bytes 491528 | tf_op jit(solution)/shard_map/ppermute | solution.py:345
  26.6 18.3 %collective-permute-start.7 = (f32[320,128]{1,0:T(8,128)S(1)}, f32[320,128]{1,0:T(8,128)S(1)}, u32[]{:S(2)}, u32[]{:S(2)}) collective-permute-start(f32[320,128]{1,0:T(8,128)S(1)} %get-tuple-element.16), channel_id=1, source_target_pairs={{0,8},{4,12},{8,16},{12,20},{16,24},{20,28},{1,9},{5,13},{9,17},{1... | collective-permute-start | bytes 491528 | tf_op jit(solution)/shard_map/ppermute | solution.py:345
  31.2 12.0 %collective-permute-start.6 = (f32[288,128]{1,0:T(8,128)S(1)}, f32[288,128]{1,0:T(8,128)S(1)}, u32[]{:S(2)}, u32[]{:S(2)}) collective-permute-start(f32[288,128]{1,0:T(8,128)S(1)} %get-tuple-element.15), channel_id=1, source_target_pairs={{0,12},{4,16},{8,20},{12,24},{16,28},{1,13},{5,17},{9,21},{13,25},... | collective-permute-start | bytes 442376 | tf_op jit(solution)/shard_map/ppermute | solution.py:345
  36.7 8.6 %collective-permute-start.9 = (f32[384,128]{1,0:T(8,128)S(1)}, f32[384,128]{1,0:T(8,128)S(1)}, u32[]{:S(2)}, u32[]{:S(2)}) collective-permute-start(f32[384,128]{1,0:T(8,128)S(1)} %get-tuple-element.17.refs_3_), channel_id=1, source_target_pairs={{4,0},{8,4},{12,8},{16,12},{20,16},{24,20},{28,24},{5,1},{9,5},{13... | collective-permute-start | bytes 589832 | tf_op jit(solution)/shard_map/ppermute | solution.py:345
  38.0 11.7 %collective-permute-start.8 = (f32[384,128]{1,0:T(8,128)S(1)}, f32[384,128]{1,0:T(8,128)S(1)}, u32[]{:S(2)}, u32[]{:S(2)}) collective-permute-start(f32[384,128]{1,0:T(8,128)S(1)} %get-tuple-element.17.refs_3_), channel_id=1, source_target_pairs={{0,4},{4,8},{8,12},{12,16},{16,20},{20,24},{24,28},{1,5},{5,9},{9,... | collective-permute-start | bytes 589832 | tf_op jit(solution)/shard_map/ppermute | solution.py:345
  43.2 12.2 %copy-start.1 = (s32[4,8192]{1,0:T(4,128)S(1)}, s32[4,8192]{1,0:T(4,128)}, u32[]{:S(2)}) copy-start(s32[4,8192]{1,0:T(4,128)} %cell_ref.3) | copy-start | bytes 393220
  43.2 12.2 %copy-start.5 = (f32[8192]{0:T(1024)S(1)}, f32[8192]{0:T(1024)}, u32[]{:S(2)}) copy-start(f32[8192]{0:T(1024)} %param.7) | copy-start | bytes 98308
  43.2 12.2 %copy-start.7 = (f32[8192]{0:T(1024)S(1)}, f32[8192]{0:T(1024)}, u32[]{:S(2)}) copy-start(f32[8192]{0:T(1024)} %param.8) | copy-start | bytes 98308
  43.3 11.9 %collective-permute-start.5 = (f32[4,32,128]{2,1,0:T(8,128)S(1)}, f32[4,32,128]{2,1,0:T(8,128)S(1)}, u32[]{:S(2)}, u32[]{:S(2)}) collective-permute-start(f32[4,32,128]{2,1,0:T(8,128)S(1)} %get-tuple-element.14.refs_0_), channel_id=1, source_target_pairs={{0,3},{1,2},{2,1},{3,0},{4,7},{5,6},{6,5},{7,4},{8,11},{9,10},{10,... | collective-permute-start | bytes 196616 | tf_op jit(solution)/shard_map/ppermute | solution.py:341
  43.3 12.1 %collective-permute-start.4 = (f32[4,32,128]{2,1,0:T(8,128)S(1)}, f32[4,32,128]{2,1,0:T(8,128)S(1)}, u32[]{:S(2)}, u32[]{:S(2)}) collective-permute-start(f32[4,32,128]{2,1,0:T(8,128)S(1)} %get-tuple-element.14.refs_0_), channel_id=1, source_target_pairs={{0,2},{1,3},{2,0},{3,1},{4,6},{5,7},{6,4},{7,5},{8,10},{9,11},{10,... | collective-permute-start | bytes 196616 | tf_op jit(solution)/shard_map/ppermute | solution.py:341
  44.9 10.5 %collective-permute-start.3 = (f32[4,32,128]{2,1,0:T(8,128)S(1)}, f32[4,32,128]{2,1,0:T(8,128)S(1)}, u32[]{:S(2)}, u32[]{:S(2)}) collective-permute-start(f32[4,32,128]{2,1,0:T(8,128)S(1)} %get-tuple-element.14.refs_0_), channel_id=1, source_target_pairs={{0,1},{1,0},{2,3},{3,2},{4,5},{5,4},{6,7},{7,6},{8,9},{9,8},{10,11... | collective-permute-start | bytes 196616 | tf_op jit(solution)/shard_map/ppermute | solution.py:341
  53.5 7.3 %copy-start.3 = (f32[3,8192]{1,0:T(4,128)S(1)}, f32[3,8192]{1,0:T(4,128)}, u32[]{:S(2)}) copy-start(f32[3,8192]{1,0:T(4,128)} %velocity_ref.1) | copy-start | bytes 294916
  53.5 5.3 %collective-permute-start.14 = (f32[6,32,128]{2,1,0:T(8,128)S(1)}, f32[6,32,128]{2,1,0:T(8,128)S(1)}, u32[]{:S(2)}, u32[]{:S(2)}) collective-permute-start(f32[6,32,128]{2,1,0:T(8,128)S(1)} %relax.1.refs_0_), channel_id=1, source_target_pairs={{0,3},{1,2},{2,1},{3,0},{4,7},{5,6},{6,5},{7,4},{8,11},{9,10},{10,... | collective-permute-start | bytes 294920 | tf_op jit(solution)/shard_map/ppermute | solution.py:341
  54.6 6.1 %collective-permute-start.13 = (f32[6,32,128]{2,1,0:T(8,128)S(1)}, f32[6,32,128]{2,1,0:T(8,128)S(1)}, u32[]{:S(2)}, u32[]{:S(2)}) collective-permute-start(f32[6,32,128]{2,1,0:T(8,128)S(1)} %relax.1.refs_0_), channel_id=1, source_target_pairs={{0,2},{1,3},{2,0},{3,1},{4,6},{5,7},{6,4},{7,5},{8,10},{9,11},{10,... | collective-permute-start | bytes 294920 | tf_op jit(solution)/shard_map/ppermute | solution.py:341
  55.2 5.6 %collective-permute-start.12 = (f32[6,32,128]{2,1,0:T(8,128)S(1)}, f32[6,32,128]{2,1,0:T(8,128)S(1)}, u32[]{:S(2)}, u32[]{:S(2)}) collective-permute-start(f32[6,32,128]{2,1,0:T(8,128)S(1)} %relax.1.refs_0_), channel_id=1, source_target_pairs={{0,1},{1,0},{2,3},{3,2},{4,5},{5,4},{6,7},{7,6},{8,9},{9,8},{10,11... | collective-permute-start | bytes 294920 | tf_op jit(solution)/shard_map/ppermute | solution.py:341
